TPU v7x, 512 devices: a whole 4x8x8 slice. The times are simulated.
512 devices in a mesh: slab: 32 (over z, y_lo), grp: 16 (over y_hi, x, core).
Axes of the slice: x: 4, y: 8 (y_hi: 2, y_lo: 4; y = y_hi * 4 + y_lo), z: 8, core: 2. Of those that a mesh axis runs over, the one named last changes fastest.
Arguments:
- particles: bfloat16 [512, 2, 256, 256], P(('slab', 'grp')), may hold values from -6 to 6
- defocus_class: int32 [512], P(('slab', 'grp')), may hold values from 0 to 15
- noise_precision: float32 [512], P(('slab', 'grp')), may hold values from 25 to 200
- live_count: int32 [16], P('grp'), may hold values from 1 to 1, as said below
- defocus: float32 [16], replicated, may hold values from 20 to 200
- reference_lines: bfloat16 [512, 2, 256], P('slab'), may hold values from -6 to 6
- line_index: int32 [16, 256, 2], replicated, may hold values from 0 to 511
- line_weight: float32 [16, 256, 2], replicated, may hold values from 0.2 to 1
- row_shifts: int32 [8], replicated, may hold values from -4 to 4
- column_shifts: int32 [8], replicated, may hold values from -4 to 4
Outputs:
- volume_sums: float32 [512, 3, 256], P(('slab', 'grp'))
- loglik: float32 [512], P(('slab', 'grp'))
Inputs may be any that keep to these rules, and one draw needn't show every extreme that they name: live_count[g] live particles occupy the first slots of each device of group g; some group is full in every draw.
All inputs are finite; a program needn't handle non-finite values.
Results may differ from a plain program's by a relative error of at most 0.0042.
Values may be sent and summed in bfloat16 or wider, within the bound.
A program may use at most 128 MiB of HBM per device.

v0:
```python
import functools
import math

import jax
import jax.numpy as jnp
from jax import lax
from jax.experimental import pallas as pl
from jax.experimental.pallas import tpu as pltpu
from jax.sharding import PartitionSpec as P

MESH = pl.DeviceIdType.MESH
EXACT = lax.Precision.HIGHEST
F32 = jnp.float32
BF16 = jnp.bfloat16
I32 = jnp.int32

NX, NY, NZ, Y_LO = 4, 8, 8, 4
SLABS = NZ * Y_LO
LINES = 512
KEEP = LINES // 2
BOX = 256
POSES = 16
GROUP = 16
WIDE = GROUP * POSES
ROWS = POSES * BOX
SHIFTS = 8


def place():
    slab = lax.axis_index("slab")
    grp = lax.axis_index("grp")
    z, y_lo = slab // Y_LO, slab % Y_LO
    y_hi, x, core = grp // (2 * NX), (grp // 2) % NX, grp % 2
    return z, y_hi * Y_LO + y_lo, x, core


def device_at(z, y, x, core):
    return (z * Y_LO + y % Y_LO, (y // Y_LO) * (2 * NX) + x * 2 + core)


def phase_angle(turns):
    signed = ((turns + BOX // 2) & (BOX - 1)) - BOX // 2
    return signed.astype(F32) * (2.0 * math.pi / BOX)


def shift_column(shifts_ref, shape):
    row = lax.broadcasted_iota(I32, shape, 0)
    column = jnp.zeros(shape, I32)
    for t in range(SHIFTS):
        column = jnp.where(row == t, shifts_ref[t], column)
    return column


def slot_of(line, z, y, x, core):
    line_y = ((line >> 3) & 1) * Y_LO + ((line >> 4) & (Y_LO - 1))
    return (
        ((line ^ core) & 1) * KEEP
        + ((((line >> 1) - x) & (NX - 1)) * (NY * NZ))
        + (((line_y - y) & (NY - 1)) * NZ)
        + (((line >> 6) - z) & (NZ - 1))
    )


def held_row(slot, z, y, x, core):
    line_z = (slot + z) & (NZ - 1)
    line_y = ((slot >> 3) + y) & (NY - 1)
    line_x = ((slot >> 6) + x) & (NX - 1)
    line_core = ((slot >> 8) ^ core) & 1
    return (line_y & 3) * (NZ * 16) + line_z * 16 + (line_y >> 2) * 8 + line_x * 2 + line_core


def expect_kernel(
    scale,
    class_ref,
    precision_ref,
    live_ref,
    defocus_ref,
    row_shift_ref,
    column_shift_ref,
    image_ref,
    index_ref,
    weight_ref,
    lines_ref,
    out_ref,
    loglik_ref,
    held,
    slots,
    weights,
    lines_t,
    spread,
    spread_low,
    slices,
    shifted,
    phases,
    squares,
    rows,
    sums,
    strided,
    pair_out,
    pair_in,
    ax_out,
    ax_in,
    by_out,
    by_in,
    cz_out,
    cz_in,
    ay_out,
    ay_in,
    bx_out,
    bx_in,
    cx_out,
    cx_in,
    last_out,
    last_in,
    gather_send,
    gather_recv,
    swap_send,
    swap_recv,
    pair_send,
    pair_recv,
    hop_send,
    hop_recv,
):
    z, y, x, core = place()
    y_lo = y % Y_LO
    sibling = device_at(z, y, x, 1 - core)

    def along_x(k):
        return device_at(z, y, (x + k) % NX, core)

    def along_y(k):
        return device_at(z, (y + NY + k) % NY, x, core)

    def along_z(k):
        return device_at((z + k) % NZ, y, x, core)

    def remote(src, dst, send, recv, device):
        return pltpu.make_async_remote_copy(
            src_ref=src,
            dst_ref=dst,
            send_sem=send,
            recv_sem=recv,
            device_id=device,
            device_id_type=MESH,
        )

    barrier = pltpu.get_barrier_semaphore()
    peers = [sibling]
    peers += [along_x(k) for k in range(1, NX)]
    peers += [along_y(k) for k in range(1, NY)]
    peers += [along_z(k) for k in range(1, NZ)]
    for peer in peers:
        pl.semaphore_signal(barrier, inc=1, device_id=peer, device_id_type=MESH)

    both = lines_ref[...]
    held[core, y_lo, z] = jnp.where(core == 0, both[:, 0, :], both[:, 1, :])

    alive = jnp.where(0 < live_ref[0], 1.0, 0.0).astype(F32)
    chosen = defocus_ref[class_ref[0]]

    lane_y = lax.broadcasted_iota(I32, (SHIFTS, BOX), 1) - BOX // 2
    angle_y = phase_angle(lane_y * shift_column(column_shift_ref, (SHIFTS, BOX)))
    cos_y = jnp.cos(angle_y)
    sin_y = jnp.sin(angle_y)
    freq_y = (lax.broadcasted_iota(I32, (GROUP, BOX), 1) - BOX // 2).astype(F32) / BOX
    row_in_group = lax.broadcasted_iota(I32, (GROUP, BOX), 0)

    def shift_rows(g, carry):
        at = pl.ds(pl.multiple_of(g * WIDE, WIDE), WIDE)
        kx = pl.ds(pl.multiple_of(g * GROUP, GROUP), GROUP)
        freq_x = (row_in_group + (g * GROUP - BOX // 2)).astype(F32) / BOX
        ctf = -jnp.sin(chosen * (freq_x * freq_x + freq_y * freq_y) + 0.1) * alive
        squares[kx, :] = ctf * ctf
        real = ctf * image_ref[0, 0, kx, :].astype(F32)
        imag = ctf * image_ref[0, 1, kx, :].astype(F32)
        blocks = []
        for k in range(GROUP):
            real_row = real[k : k + 1, :]
            imag_row = imag[k : k + 1, :]
            shift_re = real_row * cos_y + imag_row * sin_y
            shift_im = real_row * sin_y - imag_row * cos_y
            blocks.append(jnp.concatenate([shift_re, -shift_im], axis=1))
            blocks.append(jnp.concatenate([shift_im, shift_re], axis=1))
        shifted[at, :] = jnp.concatenate(blocks, axis=0).astype(BF16)
        return carry

    lax.fori_loop(0, BOX // GROUP, shift_rows, 0)

    pl.semaphore_wait(barrier, len(peers))
    gather_z = []
    for k in (4, 3, 5, 2, 6, 1, 7):
        copy = remote(
            held.at[core, y_lo, z],
            held.at[core, y_lo, z],
            gather_send.at[k],
            gather_recv.at[k],
            along_z(k),
        )
        copy.start()
        gather_z.append(copy)

    lane = lax.broadcasted_iota(I32, (SHIFTS, ROWS), 1)
    freq = (lane >> 4) - BOX // 2
    part = (lane >> 3) & 1
    turns = freq * shift_column(row_shift_ref, (SHIFTS, ROWS)) + part * (BOX // 4)
    row_phase = jnp.cos(phase_angle(turns))
    for t in range(SHIFTS):
        phases[pl.ds(t * SHIFTS, SHIFTS), :] = jnp.where((lane & 7) == t, row_phase, 0.0)

    first = slot_of(index_ref[0:1, :], z, y, x, core)
    second = slot_of(index_ref[1:2, :], z, y, x, core)
    same = first == second
    first_weight = jnp.where(same, weight_ref[0:1, :] + weight_ref[1:2, :], weight_ref[0:1, :])
    second_weight = jnp.where(same, 0.0, weight_ref[1:2, :])
    slots[0:1, :] = first
    slots[1:2, :] = second
    first_high = first_weight.astype(BF16).astype(F32)
    second_high = second_weight.astype(BF16).astype(F32)
    weights[0:1, :] = first_high
    weights[1:2, :] = second_high
    weights[2:3, :] = first_weight - first_high
    weights[3:4, :] = second_weight - second_high
    slot_row = lax.broadcasted_iota(I32, (LINES, WIDE), 0)

    def spread_rows(g, carry):
        at = pl.ds(pl.multiple_of(g * WIDE, WIDE), WIDE)
        is_first = slot_row == slots[0:1, at]
        is_second = slot_row == slots[1:2, at]
        high = jnp.where(is_first, weights[0:1, at], jnp.where(is_second, weights[1:2, at], 0.0))
        low = jnp.where(is_first, weights[2:3, at], jnp.where(is_second, weights[3:4, at], 0.0))
        spread[:, at] = high.astype(BF16)
        spread_low[:, at] = low.astype(BF16)
        return carry

    lax.fori_loop(0, 5, spread_rows, 0)
    for copy in gather_z:
        copy.wait_recv()
    far = 2 - 4 * core
    swaps = []

    def swap(d, residue):
        copy = remote(
            held.at[core, residue],
            held.at[core, residue],
            swap_send.at[d],
            swap_recv.at[d],
            sibling,
        )
        copy.start()
        swaps.append(copy)

    gather_y = []
    for d, step in ((2, far), (1, 1), (3, -1)):
        copy = remote(
            held.at[core, y_lo],
            held.at[core, y_lo],
            gather_send.at[NZ + d],
            gather_recv.at[NZ + d],
            along_y(step),
        )
        copy.start()
        gather_y.append(copy)
    swap(0, y_lo)
    lax.fori_loop(5, BOX // GROUP, spread_rows, 0)

    for copy, (d, residue) in zip(gather_y, ((2, y_lo + 2), (1, y_lo + 3), (3, y_lo + 1))):
        copy.wait_recv()
        swap(d, residue % Y_LO)

    slot_rows = held_row(lax.broadcasted_iota(I32, (1, LINES), 1), z, y, x, core)
    order = jnp.where(
        lax.broadcasted_iota(I32, (LINES, LINES), 0) == slot_rows, 1.0, 0.0
    ).astype(BF16)

    def transpose_half(c):
        lines_t[pl.ds(pl.multiple_of(c * BOX, BOX), BOX), :] = lax.dot_general(
            held[c].reshape(LINES, BOX),
            order,
            (((0,), (0,)), ((), ())),
            preferred_element_type=F32,
        ).astype(BF16)

    def slice_rows(c, at):
        half = pl.ds(pl.multiple_of(c * BOX, BOX), BOX)
        lines_half = lines_t[half, :]
        slices[half, at] = (
            jnp.dot(lines_half, spread[:, at], preferred_element_type=F32)
            + jnp.dot(lines_half, spread_low[:, at], preferred_element_type=F32)
        ).astype(BF16)

    def own_slices(g, carry):
        slice_rows(core, pl.ds(pl.multiple_of(g * WIDE, WIDE), WIDE))
        return carry

    transpose_half(core)
    lax.fori_loop(0, BOX // GROUP, own_slices, 0)
    for copy in swaps:
        copy.wait_recv()
    transpose_half(1 - core)

    one_row = (lax.broadcasted_iota(I32, (WIDE, WIDE), 0) >> 4) == (
        lax.broadcasted_iota(I32, (WIDE, WIDE), 1) >> 4
    )

    def correlate(g, corr):
        at = pl.ds(pl.multiple_of(g * WIDE, WIDE), WIDE)
        slice_rows(1 - core, at)
        products = jnp.dot(shifted[at, :], slices[:, at], preferred_element_type=F32)
        return corr + jnp.dot(
            phases[:, at],
            jnp.where(one_row, products, 0.0),
            precision=EXACT,
            preferred_element_type=F32,
        )

    corr = lax.fori_loop(
        0, BOX // GROUP, correlate, jnp.zeros((SHIFTS * SHIFTS, WIDE), F32)
    )
    corr = corr[:, : WIDE // 2] + corr[:, WIDE // 2 :]
    for step in (64, 32, 16):
        corr = corr + pltpu.roll(corr, step, 1)
    score = corr * (precision_ref[0] / BOX)
    top = jnp.max(score, axis=(0, 1), keepdims=True)
    terms = jnp.exp(score - top)
    total = jnp.sum(terms, axis=(0, 1), keepdims=True) * (1.0 / 8.0)
    posterior = terms / total
    loglik_ref[0] = ((top + jnp.log(total)) * alive)[0, 0]
    posterior_t = posterior.T
    mass = jnp.sum(posterior_t, axis=1, keepdims=True)[:POSES]

    pairs = []

    def spread_part(c):
        columns = rows[:, c * BOX : (c + 1) * BOX]
        pair_out[c] = jnp.dot(spread[KEEP:, :], columns, preferred_element_type=F32).astype(BF16)
        copy = remote(pair_out.at[c], pair_in.at[c], pair_send.at[c], pair_recv.at[c], sibling)
        copy.start()
        pairs.append(copy)
        sums[c] = jnp.dot(spread[:KEEP, :], columns, preferred_element_type=F32)

    def square_rows(g, carry):
        at = pl.ds(pl.multiple_of(g * WIDE, WIDE), WIDE)
        square = squares[pl.ds(pl.multiple_of(g * GROUP, GROUP), GROUP), :]
        rows[at, 2 * BOX :] = jnp.concatenate(
            [square[k : k + 1, :] * mass for k in range(GROUP)], axis=0
        ).astype(BF16)
        return carry

    def insert(g, carry):
        at = pl.ds(pl.multiple_of(g * WIDE, WIDE), WIDE)
        weight = jnp.dot(posterior_t, phases[:, at], precision=EXACT, preferred_element_type=F32)
        weight = jnp.where(one_row, jnp.concatenate([weight, weight], axis=0), 0.0).astype(BF16)
        rows[at, : 2 * BOX] = jnp.dot(
            weight, shifted[at, :], preferred_element_type=F32
        ).astype(BF16)
        return carry

    hops = []

    def hop(number, src, dst, device):
        copy = remote(src, dst, hop_send.at[number], hop_recv.at[number], device)
        copy.start()
        hops.append(copy)
        return copy

    def pack(piece):
        return jnp.concatenate([piece[:, :128], piece[:, 128:]], axis=0)

    def unpack(piece):
        return jnp.concatenate([piece[:NZ, :], piece[NZ:, :]], axis=1)

    ring8 = (4, 3, 5, 2, 6, 1, 7)
    ring4 = (2, 1, 3)

    lax.fori_loop(0, BOX // GROUP, square_rows, 0)
    spread_part(2)
    lax.fori_loop(0, BOX // GROUP, insert, 0)
    pairs[0].wait_recv()
    c_sum = sums[2] + pair_in[2].astype(F32)
    for half in range(2):
        strided[half] = c_sum[:, half * 128 : (half + 1) * 128]

    def c_rows(k):
        rows_k = pl.ds(k, NX * NY, NZ)
        return jnp.concatenate([strided[0, rows_k, :], strided[1, rows_k, :]], axis=1)

    c_hops = []
    for k in ring8:
        cz_out[k] = c_rows(k).astype(BF16)
        c_hops.append(hop(k, cz_out.at[k], cz_in.at[k], along_z(k)))
    spread_part(0)
    spread_part(1)

    pairs[1].wait_recv()
    b_sum = (sums[0] + pair_in[0].astype(F32)).reshape(NX, NY, NZ, BOX)
    b_hops = []
    for k in ring8:
        by_out[k] = b_sum[:, k].reshape(NX * NZ, BOX).astype(BF16)
        b_hops.append(hop(NZ + k, by_out.at[k], by_in.at[k], along_y(k)))
    b_sum = b_sum[:, 0].reshape(NX * NZ, BOX)
    pairs[2].wait_recv()
    a_sum = (sums[1] + pair_in[1].astype(F32)).reshape(NX, NY * NZ, BOX)
    a_hops = []
    for k in ring4:
        ax_out[k] = a_sum[k].astype(BF16)
        a_hops.append(hop(2 * NZ + k, ax_out.at[k], ax_in.at[k], along_x(k)))
    a_sum = a_sum[0]

    c_sum = c_rows(0)
    for k, copy in zip(ring8, c_hops):
        copy.wait_recv()
        c_sum = c_sum + cz_in[k].astype(F32)
    c_hops = []
    for k in ring4:
        cx_out[k] = pack(c_sum[k * NY : (k + 1) * NY, :]).astype(BF16)
        c_hops.append(hop(20 + k, cx_out.at[k], cx_in.at[k], along_x(k)))
    for k, copy in zip(ring8, b_hops):
        copy.wait_recv()
        b_sum = b_sum + by_in[k].astype(F32)
    b_hops = []
    for k in ring4:
        bx_out[k] = pack(b_sum[k * NZ : (k + 1) * NZ, :]).astype(BF16)
        b_hops.append(hop(24 + k, bx_out.at[k], bx_in.at[k], along_x(k)))
    for k, copy in zip(ring4, a_hops):
        copy.wait_recv()
        a_sum = a_sum + ax_in[k].astype(F32)
    a_hops = []
    for k in ring8:
        ay_out[k] = pack(a_sum[k * NZ : (k + 1) * NZ, :]).astype(BF16)
        a_hops.append(hop(28 + k, ay_out.at[k], ay_in.at[k], along_y(k)))

    def last(part, total, along):
        copies = []
        for k in ring8:
            last_out[part, k] = total[k : k + 1, :]
            copies.append(
                hop(36 + part * NZ + k, last_out.at[part, k], last_in.at[part, k], along(k))
            )
        return total[0:1, :], copies

    c_sum = c_sum[:NY, :]
    for k, copy in zip(ring4, c_hops):
        copy.wait_recv()
        c_sum = c_sum + unpack(cx_in[k].astype(F32))
    c_sum, c_hops = last(2, c_sum, along_y)
    b_sum = b_sum[:NZ, :]
    for k, copy in zip(ring4, b_hops):
        copy.wait_recv()
        b_sum = b_sum + unpack(bx_in[k].astype(F32))
    b_sum, b_hops = last(0, b_sum, along_z)
    a_sum = a_sum[:NZ, :]
    for k, copy in zip(ring8, a_hops):
        copy.wait_recv()
        a_sum = a_sum + unpack(ay_in[k].astype(F32))
    a_sum, a_hops = last(1, a_sum, along_z)
    for part, total, copies in ((2, c_sum, c_hops), (0, b_sum, b_hops), (1, a_sum, a_hops)):
        for k, copy in zip(ring8, copies):
            copy.wait_recv()
            total = total + last_in[part, k]
        out_ref[:, part * BOX : (part + 1) * BOX] = total * scale
    for copy in gather_z + gather_y + swaps + pairs + hops:
        copy.wait_send()


def expect(scale, *operands):
    smem = pl.BlockSpec(memory_space=pltpu.SMEM)
    vmem = pl.BlockSpec(memory_space=pltpu.VMEM)
    dma = pltpu.SemaphoreType.DMA
    hop_count = 36 + 3 * NZ

    def both_ways(shape, kind):
        return [pltpu.VMEM(shape, kind), pltpu.VMEM(shape, kind)]

    return pl.pallas_call(
        functools.partial(expect_kernel, scale),
        out_shape=(
            jax.ShapeDtypeStruct((1, 3 * BOX), F32),
            jax.ShapeDtypeStruct((1,), F32),
        ),
        in_specs=[smem] * 6 + [vmem] * 4,
        out_specs=(vmem, smem),
        scratch_shapes=[
            pltpu.VMEM((2, Y_LO, NZ, 16, BOX), BF16),
            pltpu.VMEM((2, ROWS), I32),
            pltpu.VMEM((4, ROWS), F32),
            pltpu.VMEM((2 * BOX, LINES), BF16),
            pltpu.VMEM((LINES, ROWS), BF16),
            pltpu.VMEM((LINES, ROWS), BF16),
            pltpu.VMEM((2 * BOX, ROWS), BF16),
            pltpu.VMEM((ROWS, 2 * BOX), BF16),
            pltpu.VMEM((SHIFTS * SHIFTS, ROWS), F32),
            pltpu.VMEM((BOX, BOX), F32),
            pltpu.VMEM((ROWS, 3 * BOX), BF16),
            pltpu.VMEM((3, KEEP, BOX), F32),
            pltpu.VMEM((2, KEEP, BOX // 2), F32),
        ]
        + both_ways((3, KEEP, BOX), BF16)
        + both_ways((NX, NY * NZ, BOX), BF16)
        + both_ways((NY, NX * NZ, BOX), BF16)
        + both_ways((NZ, NX * NY, BOX), BF16)
        + both_ways((NY, 2 * NZ, BOX // 2), BF16)
        + both_ways((NX, 2 * NZ, BOX // 2), BF16)
        + both_ways((NX, 2 * NY, BOX // 2), BF16)
        + both_ways((3, NZ, 1, BOX), F32)
        + [
            dma((NZ + Y_LO,)),
            dma((NZ + Y_LO,)),
            dma((Y_LO,)),
            dma((Y_LO,)),
            dma((3,)),
            dma((3,)),
            dma((hop_count,)),
            dma((hop_count,)),
        ],
        compiler_params=pltpu.CompilerParams(
            collective_id=0, has_side_effects=True, vmem_limit_bytes=48 * 1024 * 1024
        ),
    )(*operands)


def body(
    particles,
    defocus_class,
    noise_precision,
    live_count,
    defocus,
    reference_lines,
    line_index,
    line_weight,
    row_shifts,
    column_shifts,
):
    index = jnp.transpose(line_index, (2, 1, 0)).reshape(2, ROWS)
    weight = jnp.transpose(line_weight, (2, 1, 0)).reshape(2, ROWS)
    particle_total = particles.shape[0] * lax.axis_size("slab") * lax.axis_size("grp")
    owned, loglik = expect(
        LINES / (POSES * particle_total),
        defocus_class,
        noise_precision,
        live_count,
        defocus,
        row_shifts,
        column_shifts,
        particles,
        index,
        weight,
        reference_lines,
    )
    return owned.reshape(1, 3, BOX), loglik


def solution(mesh):
    return jax.shard_map(
        body,
        mesh=mesh,
        in_specs=(
            P(("slab", "grp"), None, None, None),
            P(("slab", "grp")),
            P(("slab", "grp")),
            P("grp"),
            P(),
            P("slab", None, None),
            P(),
            P(),
            P(),
            P(),
        ),
        out_specs=(P(("slab", "grp"), None, None), P(("slab", "grp"))),
        check_vma=False,
    )
```

profile of v0, /device:TPU:8, one launch (start us, length us, event | category | flops | bytes accessed | tf_op | source)
XLA Modules:
  0.0 83.3 jit_solution(13704548946859125605)
XLA Ops:
  0.6 0.9 %copy.15 = s32[2,256,16]{2,1,0:T(8,128)S(1)} copy(s32[2,256,16]{1,0,2:T(2,128)} %bitcast.4) | data formatting | bytes 65536 | tf_op jit(solution)/shard_map/transpose | solution.py:533
  1.5 0.0 copy-start.5
  1.5 0.2 reshape.13.index_ref
  1.7 0.6 copy-done.5
  2.3 0.0 copy-start
  2.3 0.1 copy.16
  2.4 0.0 copy-start.1
  2.4 0.2 reshape.14.weight_ref
  3.9 0.0 copy-start.2
  3.9 0.0 copy-start.3
  3.9 0.0 copy-start.4
  4.6 0.0 copy-done
  4.6 0.0 copy-done.1
  4.6 0.0 copy-done.2
  4.6 0.0 copy-done.3
  4.6 0.0 copy-done.4
  4.6 76.2 %shard_map.113 = (f32[1,768]{1,0:T(1,128)S(1)}, f32[1]{0:T(128)}) custom-call(s32[1]{0:T(128)S(6)} %copy.20.class_ref, f32[1]{0:T(128)S(6)} %copy.21.precision_ref, s32[1]{0:T(128)S(6)} %copy.22.live_ref, f32[16]{0:T(128)S(1)} %copy-done.2, s32[8]{0:T(128)S(1)} %copy-done.3, s32[8]{0:T(128)S(1)} %copy-done.4, bf16[1,2,256,256]{3,2,1,0:T(8,128)(2,1)S(1)} %copy-done, ...), custom_call_target="tpu_custom_call" | custom-call | tf_op jit(solution)/shard_map/pallas_call | solution.py:474
  80.9 0.6 copy.23
Async XLA Ops:
  1.5 0.8 copy-start.5
  2.3 2.3 %copy-start = (bf16[1,2,256,256]{3,2,1,0:T(8,128)(2,1)S(1)}, bf16[1,2,256,256]{3,2,1,0:T(8,128)(2,1)}, u32[]{:S(2)}) copy-start(bf16[1,2,256,256]{3,2,1,0:T(8,128)(2,1)} %image_ref.1) | copy-start | bytes 786436
  2.4 2.2 %copy-start.1 = (bf16[16,2,256]{2,1,0:T(2,128)(2,1)S(1)}, bf16[16,2,256]{2,1,0:T(2,128)(2,1)}, u32[]{:S(2)}) copy-start(bf16[16,2,256]{2,1,0:T(2,128)(2,1)} %lines_ref.1) | copy-start | bytes 49156
  3.9 0.7 copy-start.2
  3.9 0.7 copy-start.3
  3.9 0.7 copy-start.4
where the time goes:
time: 83.6 us; the launch traced here: 83.3 us
  Pallas kernels  76.2 us (91%)
  between operations  4.52 us (5%)
  local copies, waits for them, and re-layouts  2.52 us (3%)
    pallas_call x1, Pallas kernels, expect(): pl.pallas_call(functools.partial(expect_kernel, scale), out_shape=(jax.Sh...  76.2 us

commit v1 on v0

--- a/solution.py
+++ b/solution.py
@@ -88,11 +88,13 @@
     weights,
     lines_t,
     spread,
-    spread_low,
     slices,
     shifted,
     phases,
     squares,
+    product_high,
+    product_low,
+    turned,
     rows,
     sums,
     strided,
@@ -204,22 +206,61 @@
     part = (lane >> 3) & 1
     turns = freq * shift_column(row_shift_ref, (SHIFTS, ROWS)) + part * (BOX // 4)
     row_phase = jnp.cos(phase_angle(turns))
-    for t in range(SHIFTS):
-        phases[pl.ds(t * SHIFTS, SHIFTS), :] = jnp.where((lane & 7) == t, row_phase, 0.0)
-
-    first = slot_of(index_ref[0:1, :], z, y, x, core)
-    second = slot_of(index_ref[1:2, :], z, y, x, core)
+    row_high = row_phase.astype(BF16).astype(F32)
+    row_low = row_phase - row_high
+    for t in range(0, SHIFTS, 2):
+        for base, table in ((0, row_high), (SHIFTS * SHIFTS, row_low)):
+            phases[pl.ds(base + t * SHIFTS, 2 * SHIFTS), :] = jnp.concatenate(
+                [jnp.where((lane & 7) == t + u, table, 0.0) for u in range(2)], axis=0
+            ).astype(BF16)
+
+    first = slot_of(index_ref[:, 0, :], z, y, x, core)
+    second = slot_of(index_ref[:, 1, :], z, y, x, core)
+    first_weight = weight_ref[:, 0, :]
+    second_weight = weight_ref[:, 1, :]
     same = first == second
-    first_weight = jnp.where(same, weight_ref[0:1, :] + weight_ref[1:2, :], weight_ref[0:1, :])
-    second_weight = jnp.where(same, 0.0, weight_ref[1:2, :])
-    slots[0:1, :] = first
-    slots[1:2, :] = second
+    first_weight = jnp.where(same, first_weight + second_weight, first_weight)
+    second_weight = jnp.where(same, 0.0, second_weight)
     first_high = first_weight.astype(BF16).astype(F32)
     second_high = second_weight.astype(BF16).astype(F32)
-    weights[0:1, :] = first_high
-    weights[1:2, :] = second_high
-    weights[2:3, :] = first_weight - first_high
-    weights[3:4, :] = second_weight - second_high
+    tables = jnp.concatenate(
+        [
+            (first >> 4).astype(F32),
+            (first & 15).astype(F32),
+            (second >> 4).astype(F32),
+            (second & 15).astype(F32),
+            first_high,
+            second_high,
+            first_weight - first_high,
+            second_weight - second_high,
+        ],
+        axis=0,
+    ).astype(BF16)
+    table_lane = lax.broadcasted_iota(I32, (BOX, WIDE), 1) >> 4
+    table_row = lax.broadcasted_iota(I32, (BOX, WIDE), 0)
+    pose_row = lax.broadcasted_iota(I32, (POSES, WIDE), 0) == (
+        lax.broadcasted_iota(I32, (POSES, WIDE), 1) & (POSES - 1)
+    )
+
+    def table_rows(g, carry):
+        at = pl.ds(pl.multiple_of(g * WIDE, WIDE), WIDE)
+        chosen_row = jnp.where(table_row == table_lane + g * GROUP, 1.0, 0.0).astype(BF16)
+        wide = jnp.dot(tables, chosen_row, preferred_element_type=F32)
+        found = [
+            jnp.sum(
+                jnp.where(pose_row, wide[n * POSES : (n + 1) * POSES, :], 0.0),
+                axis=0,
+                keepdims=True,
+            )
+            for n in range(8)
+        ]
+        slots[0:1, at] = (found[0] * 16.0 + found[1]).astype(I32)
+        slots[1:2, at] = (found[2] * 16.0 + found[3]).astype(I32)
+        for n in range(4):
+            weights[n : n + 1, at] = found[4 + n]
+        return carry
+
+    lax.fori_loop(0, BOX // GROUP, table_rows, 0, unroll=2)
     slot_row = lax.broadcasted_iota(I32, (LINES, WIDE), 0)
 
     def spread_rows(g, carry):
@@ -228,8 +269,8 @@
         is_second = slot_row == slots[1:2, at]
         high = jnp.where(is_first, weights[0:1, at], jnp.where(is_second, weights[1:2, at], 0.0))
         low = jnp.where(is_first, weights[2:3, at], jnp.where(is_second, weights[3:4, at], 0.0))
-        spread[:, at] = high.astype(BF16)
-        spread_low[:, at] = low.astype(BF16)
+        spread[:LINES, at] = high.astype(BF16)
+        spread[LINES:, at] = low.astype(BF16)
         return carry
 
     lax.fori_loop(0, 5, spread_rows, 0)
@@ -273,48 +314,61 @@
     ).astype(BF16)
 
     def transpose_half(c):
-        lines_t[pl.ds(pl.multiple_of(c * BOX, BOX), BOX), :] = lax.dot_general(
+        half = lax.dot_general(
             held[c].reshape(LINES, BOX),
             order,
             (((0,), (0,)), ((), ())),
             preferred_element_type=F32,
         ).astype(BF16)
-
-    def slice_rows(c, at):
+        lines_t[pl.ds(pl.multiple_of(c * BOX, BOX), BOX), :] = jnp.concatenate(
+            [half, half], axis=1
+        )
+
+    def slice_half(c):
         half = pl.ds(pl.multiple_of(c * BOX, BOX), BOX)
-        lines_half = lines_t[half, :]
-        slices[half, at] = (
-            jnp.dot(lines_half, spread[:, at], preferred_element_type=F32)
-            + jnp.dot(lines_half, spread_low[:, at], preferred_element_type=F32)
-        ).astype(BF16)
-
-    def own_slices(g, carry):
-        slice_rows(core, pl.ds(pl.multiple_of(g * WIDE, WIDE), WIDE))
+
+        def step(n, carry):
+            at = pl.ds(pl.multiple_of(n * 4 * WIDE, 4 * WIDE), 4 * WIDE)
+            slices[half, at] = jnp.dot(
+                lines_t[half, :], spread[:, at], preferred_element_type=F32
+            ).astype(BF16)
+            return carry
+
+        lax.fori_loop(0, ROWS // (4 * WIDE), step, 0)
+
+    transpose_half(core)
+    slice_half(core)
+    for copy in swaps:
+        copy.wait_recv()
+    transpose_half(1 - core)
+    slice_half(1 - core)
+
+    lane_row = lax.broadcasted_iota(I32, (GROUP, 128), 1) >> 4
+    nothing = jnp.zeros((GROUP, 128), BF16)
+
+    def diagonal(k, tile):
+        return jnp.concatenate([tile, nothing] if k < GROUP // 2 else [nothing, tile], axis=1)
+
+    def correlate(g, carry):
+        at = pl.ds(pl.multiple_of(g * WIDE, WIDE), WIDE)
+        products = jnp.dot(shifted[at, :], slices[:, at], preferred_element_type=F32)
+        highs, lows = [], []
+        for k in range(GROUP):
+            lane_at = k // (GROUP // 2) * 128
+            block = products[k * GROUP : (k + 1) * GROUP, lane_at : lane_at + 128]
+            block = jnp.where(lane_row == k % (GROUP // 2), block, 0.0)
+            high = block.astype(BF16)
+            highs.append(diagonal(k, high))
+            lows.append(diagonal(k, (block - high.astype(F32)).astype(BF16)))
+        product_high[at, :] = jnp.concatenate(highs, axis=0)
+        product_low[at, :] = jnp.concatenate(lows, axis=0)
         return carry
 
-    transpose_half(core)
-    lax.fori_loop(0, BOX // GROUP, own_slices, 0)
-    for copy in swaps:
-        copy.wait_recv()
-    transpose_half(1 - core)
-
-    one_row = (lax.broadcasted_iota(I32, (WIDE, WIDE), 0) >> 4) == (
-        lax.broadcasted_iota(I32, (WIDE, WIDE), 1) >> 4
-    )
-
-    def correlate(g, corr):
-        at = pl.ds(pl.multiple_of(g * WIDE, WIDE), WIDE)
-        slice_rows(1 - core, at)
-        products = jnp.dot(shifted[at, :], slices[:, at], preferred_element_type=F32)
-        return corr + jnp.dot(
-            phases[:, at],
-            jnp.where(one_row, products, 0.0),
-            precision=EXACT,
-            preferred_element_type=F32,
-        )
-
-    corr = lax.fori_loop(
-        0, BOX // GROUP, correlate, jnp.zeros((SHIFTS * SHIFTS, WIDE), F32)
+    lax.fori_loop(0, BOX // GROUP, correlate, 0, unroll=4)
+    corr = jnp.dot(phases[...], product_high[...], preferred_element_type=F32)
+    corr = corr[: SHIFTS * SHIFTS] + corr[SHIFTS * SHIFTS :]
+    corr = corr + jnp.dot(
+        phases[: SHIFTS * SHIFTS, :], product_low[...], preferred_element_type=F32
     )
     corr = corr[:, : WIDE // 2] + corr[:, WIDE // 2 :]
     for step in (64, 32, 16):
@@ -325,14 +379,14 @@
     total = jnp.sum(terms, axis=(0, 1), keepdims=True) * (1.0 / 8.0)
     posterior = terms / total
     loglik_ref[0] = ((top + jnp.log(total)) * alive)[0, 0]
-    posterior_t = posterior.T
-    mass = jnp.sum(posterior_t, axis=1, keepdims=True)[:POSES]
+    posterior_t = posterior.T[:POSES]
+    mass = jnp.sum(posterior_t, axis=1, keepdims=True)
 
     pairs = []
 
     def spread_part(c):
         columns = rows[:, c * BOX : (c + 1) * BOX]
-        pair_out[c] = jnp.dot(spread[KEEP:, :], columns, preferred_element_type=F32).astype(BF16)
+        pair_out[c] = jnp.dot(spread[KEEP:LINES, :], columns, preferred_element_type=F32).astype(BF16)
         copy = remote(pair_out.at[c], pair_in.at[c], pair_send.at[c], pair_recv.at[c], sibling)
         copy.start()
         pairs.append(copy)
@@ -346,10 +400,36 @@
         ).astype(BF16)
         return carry
 
+    def turn_poses():
+        high = posterior_t.astype(BF16)
+        low = (posterior_t - high.astype(F32)).astype(BF16)
+        parts = jnp.concatenate(
+            [
+                jnp.concatenate([high, high], axis=1),
+                jnp.concatenate([low, jnp.zeros_like(low)], axis=1),
+            ],
+            axis=0,
+        )
+        both_parts = jnp.dot(parts, phases[...], preferred_element_type=F32)
+        turned[...] = (both_parts[:POSES] + both_parts[POSES:]).astype(BF16)
+
     def insert(g, carry):
         at = pl.ds(pl.multiple_of(g * WIDE, WIDE), WIDE)
-        weight = jnp.dot(posterior_t, phases[:, at], precision=EXACT, preferred_element_type=F32)
-        weight = jnp.where(one_row, jnp.concatenate([weight, weight], axis=0), 0.0).astype(BF16)
+        turns_g = turned[:, at]
+        weight = jnp.concatenate(
+            [
+                diagonal(
+                    k,
+                    jnp.where(
+                        lane_row == k % (GROUP // 2),
+                        turns_g[:, k // (GROUP // 2) * 128 : k // (GROUP // 2) * 128 + 128],
+                        nothing,
+                    ),
+                )
+                for k in range(GROUP)
+            ],
+            axis=0,
+        )
         rows[at, : 2 * BOX] = jnp.dot(
             weight, shifted[at, :], preferred_element_type=F32
         ).astype(BF16)
@@ -372,9 +452,10 @@
     ring8 = (4, 3, 5, 2, 6, 1, 7)
     ring4 = (2, 1, 3)
 
-    lax.fori_loop(0, BOX // GROUP, square_rows, 0)
+    lax.fori_loop(0, BOX // GROUP, square_rows, 0, unroll=2)
     spread_part(2)
-    lax.fori_loop(0, BOX // GROUP, insert, 0)
+    turn_poses()
+    lax.fori_loop(0, BOX // GROUP, insert, 0, unroll=4)
     pairs[0].wait_recv()
     c_sum = sums[2] + pair_in[2].astype(F32)
     for half in range(2):
@@ -483,13 +564,15 @@
             pltpu.VMEM((2, Y_LO, NZ, 16, BOX), BF16),
             pltpu.VMEM((2, ROWS), I32),
             pltpu.VMEM((4, ROWS), F32),
-            pltpu.VMEM((2 * BOX, LINES), BF16),
-            pltpu.VMEM((LINES, ROWS), BF16),
-            pltpu.VMEM((LINES, ROWS), BF16),
+            pltpu.VMEM((2 * BOX, 2 * LINES), BF16),
+            pltpu.VMEM((2 * LINES, ROWS), BF16),
             pltpu.VMEM((2 * BOX, ROWS), BF16),
             pltpu.VMEM((ROWS, 2 * BOX), BF16),
-            pltpu.VMEM((SHIFTS * SHIFTS, ROWS), F32),
+            pltpu.VMEM((2 * SHIFTS * SHIFTS, ROWS), BF16),
             pltpu.VMEM((BOX, BOX), F32),
+            pltpu.VMEM((ROWS, WIDE), BF16),
+            pltpu.VMEM((ROWS, WIDE), BF16),
+            pltpu.VMEM((POSES, ROWS), BF16),
             pltpu.VMEM((ROWS, 3 * BOX), BF16),
             pltpu.VMEM((3, KEEP, BOX), F32),
             pltpu.VMEM((2, KEEP, BOX // 2), F32),
@@ -530,8 +613,8 @@
     row_shifts,
     column_shifts,
 ):
-    index = jnp.transpose(line_index, (2, 1, 0)).reshape(2, ROWS)
-    weight = jnp.transpose(line_weight, (2, 1, 0)).reshape(2, ROWS)
+    index = jnp.transpose(line_index, (0, 2, 1))
+    weight = jnp.transpose(line_weight, (0, 2, 1))
     particle_total = particles.shape[0] * lax.axis_size("slab") * lax.axis_size("grp")
     owned, loglik = expect(
         LINES / (POSES * particle_total),

time: 83.6 us -> 66.2 us (0.79)
  Pallas kernels: 76.2 us -> 57.1 us
  local copies, waits for them, and re-layouts: 2.52 us -> 4.42 us
    pallas_call x1, Pallas kernels: 76.2 us -> 57.1 us  [expect(): pl.pallas_call(functools.partial(expect_kernel, scale), out_shape=(jax.Sh...]
    unnamed x13 -> x15, local copies, waits for them, and re-layouts: 1.21 us -> 4.42 us
    transpose x2 -> x0, local copies, waits for them, and re-layouts: 1.01 us -> none  [the longest x1 0.88 us: body(): index = jnp.transpose(line_index, (2, 1, 0)).reshape(2, ROWS)]
where the time goes in v1:
time: 66.2 us; the launch traced here: 65.8 us
  Pallas kernels  57.1 us (86%)
  local copies, waits for them, and re-layouts  4.42 us (7%)
  between operations  4.3 us (6%)
    pallas_call x1, Pallas kernels, expect(): pl.pallas_call(functools.partial(expect_kernel, scale), out_shape=(jax.Sh...  57.1 us
    unnamed x15, local copies, waits for them, and re-layouts  4.42 us

profile of v1, /device:TPU:8, one launch (start us, length us, event | category | flops | bytes accessed | tf_op | source)
XLA Modules:
  0.0 65.8 jit_solution(18204368961316613409)
XLA Ops:
  2.6 0.0 copy-start.4
  2.6 0.0 copy-start.5
  2.6 0.0 copy-start.6
  2.6 0.6 copy-done.4
  3.2 0.0 copy-done.5
  3.2 0.0 copy-done.6
  3.3 0.0 copy-start
  3.3 0.9 %copy-done = bf16[1,2,256,256]{3,2,1,0:T(8,128)(2,1)S(1)} copy-done((bf16[1,2,256,256]{3,2,1,0:T(8,128)(2,1)S(1)}, bf16[1,2,256,256]{3,2,1,0:T(8,128)(2,1)}, u32[]{:S(2)}) %copy-start) | copy-done | bytes 262168
  4.2 0.0 copy-start.1
  4.2 0.8 %copy-done.1 = s32[16,256,2]{1,2,0:T(2,128)S(1)} copy-done((s32[16,256,2]{1,2,0:T(2,128)S(1)}, s32[16,256,2]{1,2,0:T(2,128)}, u32[]{:S(2)}) %copy-start.1) | copy-done | bytes 32792
  5.0 0.0 copy-start.2
  5.0 0.8 %copy-done.2 = f32[16,256,2]{1,2,0:T(2,128)S(1)} copy-done((f32[16,256,2]{1,2,0:T(2,128)S(1)}, f32[16,256,2]{1,2,0:T(2,128)}, u32[]{:S(2)}) %copy-start.2) | copy-done | bytes 32792
  5.7 0.0 copy-start.3
  5.7 0.7 %copy-done.3 = bf16[16,2,256]{2,1,0:T(2,128)(2,1)S(1)} copy-done((bf16[16,2,256]{2,1,0:T(2,128)(2,1)S(1)}, bf16[16,2,256]{2,1,0:T(2,128)(2,1)}, u32[]{:S(2)}) %copy-start.3) | copy-done | bytes 16408
  6.4 57.1 %shard_map.113 = (f32[1,768]{1,0:T(1,128)S(1)}, f32[1]{0:T(128)}) custom-call(s32[1]{0:T(128)S(6)} %copy.16.class_ref, f32[1]{0:T(128)S(6)} %copy.17.precision_ref, s32[1]{0:T(128)S(6)} %copy.18.live_ref, f32[16]{0:T(128)S(1)} %copy-done.4, s32[8]{0:T(128)S(1)} %copy-done.5, s32[8]{0:T(128)S(1)} %copy-done.6, bf16[1,2,256,256]{3,2,1,0:T(8,128)(2,1)S(1)} %copy-done, ...), custom_call_target="tpu_custom_call" | custom-call | tf_op jit(solution)/shard_map/pallas_call | solution.py:555
  63.5 0.6 copy.19
Async XLA Ops:
  2.6 0.7 copy-start.4
  2.6 0.7 %copy-start.5 = (s32[8]{0:T(128)S(1)}, s32[8]{0:T(128)}, u32[]{:S(2)}) copy-start(s32[8]{0:T(128)} %row_shift_ref.1) | copy-start | bytes 100
  2.6 0.7 %copy-start.6 = (s32[8]{0:T(128)S(1)}, s32[8]{0:T(128)}, u32[]{:S(2)}) copy-start(s32[8]{0:T(128)} %column_shift_ref.1) | copy-start | bytes 100
  3.3 0.9 %copy-start = (bf16[1,2,256,256]{3,2,1,0:T(8,128)(2,1)S(1)}, bf16[1,2,256,256]{3,2,1,0:T(8,128)(2,1)}, u32[]{:S(2)}) copy-start(bf16[1,2,256,256]{3,2,1,0:T(8,128)(2,1)} %image_ref.1) | copy-start | bytes 786436
  4.2 0.8 %copy-start.1 = (s32[16,256,2]{1,2,0:T(2,128)S(1)}, s32[16,256,2]{1,2,0:T(2,128)}, u32[]{:S(2)}) copy-start(s32[16,256,2]{1,2,0:T(2,128)} %param.16) | copy-start | bytes 98308
  5.0 0.8 %copy-start.2 = (f32[16,256,2]{1,2,0:T(2,128)S(1)}, f32[16,256,2]{1,2,0:T(2,128)}, u32[]{:S(2)}) copy-start(f32[16,256,2]{1,2,0:T(2,128)} %param.17) | copy-start | bytes 98308
  5.7 0.7 %copy-start.3 = (bf16[16,2,256]{2,1,0:T(2,128)(2,1)S(1)}, bf16[16,2,256]{2,1,0:T(2,128)(2,1)}, u32[]{:S(2)}) copy-start(bf16[16,2,256]{2,1,0:T(2,128)(2,1)} %lines_ref.1) | copy-start | bytes 49156

commit v2 on v1

--- a/solution.py
+++ b/solution.py
@@ -71,6 +71,18 @@
 
 def expect_kernel(
     scale,
+    class_hbm,
+    precision_hbm,
+    live_hbm,
+    defocus_hbm,
+    row_shift_hbm,
+    column_shift_hbm,
+    image_hbm,
+    index_hbm,
+    weight_hbm,
+    lines_hbm,
+    out_ref,
+    loglik_ref,
     class_ref,
     precision_ref,
     live_ref,
@@ -81,8 +93,7 @@
     index_ref,
     weight_ref,
     lines_ref,
-    out_ref,
-    loglik_ref,
+    load_sem,
     held,
     slots,
     weights,
@@ -106,23 +117,39 @@
     by_in,
     cz_out,
     cz_in,
-    ay_out,
-    ay_in,
-    bx_out,
-    bx_in,
-    cx_out,
-    cx_in,
-    last_out,
-    last_in,
+    a_last_out,
+    a_last_in,
+    b_last_out,
+    b_last_in,
+    c_last_out,
+    c_last_in,
     gather_send,
     gather_recv,
-    swap_send,
-    swap_recv,
     pair_send,
     pair_recv,
     hop_send,
     hop_recv,
+    ready,
 ):
+    loads = [
+        pltpu.make_async_copy(src, dst, load_sem.at[n])
+        for n, (src, dst) in enumerate(
+            [
+                (lines_hbm, lines_ref),
+                (class_hbm, class_ref),
+                (live_hbm, live_ref),
+                (defocus_hbm, defocus_ref),
+                (column_shift_hbm, column_shift_ref),
+                (row_shift_hbm, row_shift_ref),
+                (image_hbm, image_ref),
+                (index_hbm, index_ref),
+                (weight_hbm, weight_ref),
+                (precision_hbm, precision_ref),
+            ]
+        )
+    ]
+    for load in loads:
+        load.start()
     z, y, x, core = place()
     y_lo = y % Y_LO
     sibling = device_at(z, y, x, 1 - core)
@@ -154,8 +181,50 @@
     for peer in peers:
         pl.semaphore_signal(barrier, inc=1, device_id=peer, device_id_type=MESH)
 
+    loads[0].wait()
     both = lines_ref[...]
     held[core, y_lo, z] = jnp.where(core == 0, both[:, 0, :], both[:, 1, :])
+
+    pl.semaphore_wait(barrier, len(peers))
+    for k in range(1, NX):
+        pl.semaphore_signal(ready, inc=1, device_id=along_x(k), device_id_type=MESH)
+    sent = []
+
+    def send_block(src, number, device):
+        copy = remote(src, src, gather_send.at[number], gather_recv.at[number], device)
+        copy.start()
+        sent.append(copy)
+        return copy
+
+    near_z = {
+        k: send_block(held.at[core, y_lo, z], k, along_z(k)) for k in (4, 3, 5, 2, 6, 1, 7)
+    }
+    far = 2 - 4 * core
+    steps = {1: 1, 2: far, 3: -1}
+    near_y = {}
+    swaps = []
+
+    def pass_along_y(k):
+        block = held.at[core, y_lo, (z + NZ - k) % NZ]
+        for d in (2, 1, 3):
+            near_y[d, k] = send_block(block, 8 * d + k, along_y(steps[d]))
+        swaps.append(send_block(block, 32 + k, sibling))
+
+    def pass_on(*distances):
+        for k in distances:
+            near_z[k].wait_recv()
+            pass_along_y(k)
+
+    def swap(*distances):
+        for k in distances:
+            for d, residue in ((1, y_lo + 3), (3, y_lo + 1), (2, y_lo + 2)):
+                near_y[d, k].wait_recv()
+                block = held.at[core, residue % Y_LO, (z + NZ - k) % NZ]
+                swaps.append(send_block(block, 32 + 8 * d + k, sibling))
+
+    pass_along_y(0)
+    for load in loads[1:]:
+        load.wait()
 
     alive = jnp.where(0 < live_ref[0], 1.0, 0.0).astype(F32)
     chosen = defocus_ref[class_ref[0]]
@@ -188,19 +257,6 @@
 
     lax.fori_loop(0, BOX // GROUP, shift_rows, 0)
 
-    pl.semaphore_wait(barrier, len(peers))
-    gather_z = []
-    for k in (4, 3, 5, 2, 6, 1, 7):
-        copy = remote(
-            held.at[core, y_lo, z],
-            held.at[core, y_lo, z],
-            gather_send.at[k],
-            gather_recv.at[k],
-            along_z(k),
-        )
-        copy.start()
-        gather_z.append(copy)
-
     lane = lax.broadcasted_iota(I32, (SHIFTS, ROWS), 1)
     freq = (lane >> 4) - BOX // 2
     part = (lane >> 3) & 1
@@ -214,6 +270,7 @@
                 [jnp.where((lane & 7) == t + u, table, 0.0) for u in range(2)], axis=0
             ).astype(BF16)
 
+    pass_on(1, 7)
     first = slot_of(index_ref[:, 0, :], z, y, x, core)
     second = slot_of(index_ref[:, 1, :], z, y, x, core)
     first_weight = weight_ref[:, 0, :]
@@ -260,7 +317,10 @@
             weights[n : n + 1, at] = found[4 + n]
         return carry
 
-    lax.fori_loop(0, BOX // GROUP, table_rows, 0, unroll=2)
+    lax.fori_loop(0, 8, table_rows, 0, unroll=2)
+    pass_on(2, 6)
+    lax.fori_loop(8, BOX // GROUP, table_rows, 0, unroll=2)
+    pass_on(3, 5, 4)
     slot_row = lax.broadcasted_iota(I32, (LINES, WIDE), 0)
 
     def spread_rows(g, carry):
@@ -274,39 +334,11 @@
         return carry
 
     lax.fori_loop(0, 5, spread_rows, 0)
-    for copy in gather_z:
-        copy.wait_recv()
-    far = 2 - 4 * core
-    swaps = []
-
-    def swap(d, residue):
-        copy = remote(
-            held.at[core, residue],
-            held.at[core, residue],
-            swap_send.at[d],
-            swap_recv.at[d],
-            sibling,
-        )
-        copy.start()
-        swaps.append(copy)
-
-    gather_y = []
-    for d, step in ((2, far), (1, 1), (3, -1)):
-        copy = remote(
-            held.at[core, y_lo],
-            held.at[core, y_lo],
-            gather_send.at[NZ + d],
-            gather_recv.at[NZ + d],
-            along_y(step),
-        )
-        copy.start()
-        gather_y.append(copy)
-    swap(0, y_lo)
-    lax.fori_loop(5, BOX // GROUP, spread_rows, 0)
-
-    for copy, (d, residue) in zip(gather_y, ((2, y_lo + 2), (1, y_lo + 3), (3, y_lo + 1))):
-        copy.wait_recv()
-        swap(d, residue % Y_LO)
+    swap(0, 1, 7)
+    lax.fori_loop(5, 10, spread_rows, 0)
+    swap(2, 6)
+    lax.fori_loop(10, BOX // GROUP, spread_rows, 0)
+    swap(3, 5, 4)
 
     slot_rows = held_row(lax.broadcasted_iota(I32, (1, LINES), 1), z, y, x, core)
     order = jnp.where(
@@ -334,7 +366,7 @@
             ).astype(BF16)
             return carry
 
-        lax.fori_loop(0, ROWS // (4 * WIDE), step, 0)
+        lax.fori_loop(0, ROWS // (4 * WIDE), step, 0, unroll=True)
 
     transpose_half(core)
     slice_half(core)
@@ -443,12 +475,6 @@
         hops.append(copy)
         return copy
 
-    def pack(piece):
-        return jnp.concatenate([piece[:, :128], piece[:, 128:]], axis=0)
-
-    def unpack(piece):
-        return jnp.concatenate([piece[:NZ, :], piece[NZ:, :]], axis=1)
-
     ring8 = (4, 3, 5, 2, 6, 1, 7)
     ring4 = (2, 1, 3)
 
@@ -487,59 +513,58 @@
         a_hops.append(hop(2 * NZ + k, ax_out.at[k], ax_in.at[k], along_x(k)))
     a_sum = a_sum[0]
 
+    pl.semaphore_wait(ready, NX - 1)
+
+    def last(rows_out, rows_in, total, number, owner):
+        count = total.shape[0]
+        rows_out[...] = total.reshape(count, 1, BOX)
+        copies = []
+        for n in range(count - 1, 0, -1):
+            copies.append(
+                hop(number + n, rows_out.at[n], rows_in.at[n], owner(n))
+            )
+        return copies
+
+    def collect(rows_in, total, copies):
+        for copy in copies:
+            copy.wait_recv()
+        return total[0:1, :] + jnp.sum(rows_in[1:], axis=0)
+
     c_sum = c_rows(0)
     for k, copy in zip(ring8, c_hops):
         copy.wait_recv()
         c_sum = c_sum + cz_in[k].astype(F32)
-    c_hops = []
-    for k in ring4:
-        cx_out[k] = pack(c_sum[k * NY : (k + 1) * NY, :]).astype(BF16)
-        c_hops.append(hop(20 + k, cx_out.at[k], cx_in.at[k], along_x(k)))
+    c_hops = last(
+        c_last_out,
+        c_last_in,
+        c_sum,
+        20,
+        lambda n: device_at(z, (y + n % NY) % NY, (x + n // NY) % NX, core),
+    )
+    for k, copy in zip(ring4, a_hops):
+        copy.wait_recv()
+        a_sum = a_sum + ax_in[k].astype(F32)
+    a_hops = last(
+        a_last_out,
+        a_last_in,
+        a_sum,
+        52,
+        lambda n: device_at((z + n % NZ) % NZ, (y + n // NZ) % NY, x, core),
+    )
     for k, copy in zip(ring8, b_hops):
         copy.wait_recv()
         b_sum = b_sum + by_in[k].astype(F32)
-    b_hops = []
-    for k in ring4:
-        bx_out[k] = pack(b_sum[k * NZ : (k + 1) * NZ, :]).astype(BF16)
-        b_hops.append(hop(24 + k, bx_out.at[k], bx_in.at[k], along_x(k)))
-    for k, copy in zip(ring4, a_hops):
-        copy.wait_recv()
-        a_sum = a_sum + ax_in[k].astype(F32)
-    a_hops = []
-    for k in ring8:
-        ay_out[k] = pack(a_sum[k * NZ : (k + 1) * NZ, :]).astype(BF16)
-        a_hops.append(hop(28 + k, ay_out.at[k], ay_in.at[k], along_y(k)))
-
-    def last(part, total, along):
-        copies = []
-        for k in ring8:
-            last_out[part, k] = total[k : k + 1, :]
-            copies.append(
-                hop(36 + part * NZ + k, last_out.at[part, k], last_in.at[part, k], along(k))
-            )
-        return total[0:1, :], copies
-
-    c_sum = c_sum[:NY, :]
-    for k, copy in zip(ring4, c_hops):
-        copy.wait_recv()
-        c_sum = c_sum + unpack(cx_in[k].astype(F32))
-    c_sum, c_hops = last(2, c_sum, along_y)
-    b_sum = b_sum[:NZ, :]
-    for k, copy in zip(ring4, b_hops):
-        copy.wait_recv()
-        b_sum = b_sum + unpack(bx_in[k].astype(F32))
-    b_sum, b_hops = last(0, b_sum, along_z)
-    a_sum = a_sum[:NZ, :]
-    for k, copy in zip(ring8, a_hops):
-        copy.wait_recv()
-        a_sum = a_sum + unpack(ay_in[k].astype(F32))
-    a_sum, a_hops = last(1, a_sum, along_z)
-    for part, total, copies in ((2, c_sum, c_hops), (0, b_sum, b_hops), (1, a_sum, a_hops)):
-        for k, copy in zip(ring8, copies):
-            copy.wait_recv()
-            total = total + last_in[part, k]
-        out_ref[:, part * BOX : (part + 1) * BOX] = total * scale
-    for copy in gather_z + gather_y + swaps + pairs + hops:
+    b_hops = last(
+        b_last_out,
+        b_last_in,
+        b_sum,
+        116,
+        lambda n: device_at((z + n % NZ) % NZ, y, (x + n // NZ) % NX, core),
+    )
+    out_ref[:, 2 * BOX :] = collect(c_last_in, c_sum, c_hops) * scale
+    out_ref[:, BOX : 2 * BOX] = collect(a_last_in, a_sum, a_hops) * scale
+    out_ref[:, :BOX] = collect(b_last_in, b_sum, b_hops) * scale
+    for copy in sent + pairs + hops:
         copy.wait_send()
 
 
@@ -547,7 +572,7 @@
     smem = pl.BlockSpec(memory_space=pltpu.SMEM)
     vmem = pl.BlockSpec(memory_space=pltpu.VMEM)
     dma = pltpu.SemaphoreType.DMA
-    hop_count = 36 + 3 * NZ
+    hop_count = 116 + NX * NZ
 
     def both_ways(shape, kind):
         return [pltpu.VMEM(shape, kind), pltpu.VMEM(shape, kind)]
@@ -558,9 +583,14 @@
             jax.ShapeDtypeStruct((1, 3 * BOX), F32),
             jax.ShapeDtypeStruct((1,), F32),
         ),
-        in_specs=[smem] * 6 + [vmem] * 4,
+        in_specs=[pl.BlockSpec(memory_space=pltpu.HBM)] * 10,
         out_specs=(vmem, smem),
         scratch_shapes=[
+            pltpu.SMEM(operand.shape, operand.dtype) for operand in operands[:6]
+        ]
+        + [pltpu.VMEM(operand.shape, operand.dtype) for operand in operands[6:]]
+        + [dma((10,))]
+        + [
             pltpu.VMEM((2, Y_LO, NZ, 16, BOX), BF16),
             pltpu.VMEM((2, ROWS), I32),
             pltpu.VMEM((4, ROWS), F32),
@@ -581,19 +611,17 @@
         + both_ways((NX, NY * NZ, BOX), BF16)
         + both_ways((NY, NX * NZ, BOX), BF16)
         + both_ways((NZ, NX * NY, BOX), BF16)
-        + both_ways((NY, 2 * NZ, BOX // 2), BF16)
-        + both_ways((NX, 2 * NZ, BOX // 2), BF16)
-        + both_ways((NX, 2 * NY, BOX // 2), BF16)
-        + both_ways((3, NZ, 1, BOX), F32)
+        + both_ways((NY * NZ, 1, BOX), F32)
+        + both_ways((NX * NZ, 1, BOX), F32)
+        + both_ways((NX * NY, 1, BOX), F32)
         + [
-            dma((NZ + Y_LO,)),
-            dma((NZ + Y_LO,)),
-            dma((Y_LO,)),
-            dma((Y_LO,)),
+            dma((2 * SLABS,)),
+            dma((2 * SLABS,)),
             dma((3,)),
             dma((3,)),
             dma((hop_count,)),
             dma((hop_count,)),
+            pltpu.SemaphoreType.REGULAR,
         ],
         compiler_params=pltpu.CompilerParams(
             collective_id=0, has_side_effects=True, vmem_limit_bytes=48 * 1024 * 1024

time: 66.2 us -> 67.4 us (1.018)
  the two profiles are of different devices: /device:TPU:8 before, /device:TPU:1 now
where the time goes in v2:
time: 67.4 us; the launch traced here: 67 us
  Pallas kernels  58.3 us (86%)
  local copies, waits for them, and re-layouts  4.42 us (7%)
  between operations  4.3 us (6%)
    pallas_call x1, Pallas kernels, expect(): pl.pallas_call(functools.partial(expect_kernel, scale), out_shape=(jax.Sh...  58.3 us
    unnamed x15, local copies, waits for them, and re-layouts  4.42 us

profile of v2, /device:TPU:1, one launch (start us, length us, event | category | flops | bytes accessed | tf_op | source)
XLA Modules:
  0.0 67.0 jit_solution(14195044843270396963)
XLA Ops:
  2.6 0.0 copy-start.4
  2.6 0.0 copy-start.5
  2.6 0.0 copy-start.6
  2.6 0.6 copy-done.4
  3.2 0.0 copy-done.5
  3.2 0.0 copy-done.6
  3.3 0.0 copy-start
  3.3 0.9 %copy-done = bf16[1,2,256,256]{3,2,1,0:T(8,128)(2,1)S(1)} copy-done((bf16[1,2,256,256]{3,2,1,0:T(8,128)(2,1)S(1)}, bf16[1,2,256,256]{3,2,1,0:T(8,128)(2,1)}, u32[]{:S(2)}) %copy-start) | copy-done | bytes 262168
  4.2 0.0 copy-start.1
  4.2 0.8 %copy-done.1 = s32[16,256,2]{1,2,0:T(2,128)S(1)} copy-done((s32[16,256,2]{1,2,0:T(2,128)S(1)}, s32[16,256,2]{1,2,0:T(2,128)}, u32[]{:S(2)}) %copy-start.1) | copy-done | bytes 32792
  5.0 0.0 copy-start.2
  5.0 0.8 %copy-done.2 = f32[16,256,2]{1,2,0:T(2,128)S(1)} copy-done((f32[16,256,2]{1,2,0:T(2,128)S(1)}, f32[16,256,2]{1,2,0:T(2,128)}, u32[]{:S(2)}) %copy-start.2) | copy-done | bytes 32792
  5.7 0.0 copy-start.3
  5.7 0.7 %copy-done.3 = bf16[16,2,256]{2,1,0:T(2,128)(2,1)S(1)} copy-done((bf16[16,2,256]{2,1,0:T(2,128)(2,1)S(1)}, bf16[16,2,256]{2,1,0:T(2,128)(2,1)}, u32[]{:S(2)}) %copy-start.3) | copy-done | bytes 16408
  6.4 58.3 %shard_map.113 = (f32[1,768]{1,0:T(1,128)S(1)}, f32[1]{0:T(128)}) custom-call(s32[1]{0:T(128)S(6)} %copy.16.class_hbm, f32[1]{0:T(128)S(6)} %copy.17.precision_hbm, s32[1]{0:T(128)S(6)} %copy.18.live_hbm, f32[16]{0:T(128)S(1)} %copy-done.4, s32[8]{0:T(128)S(1)} %copy-done.5, s32[8]{0:T(128)S(1)} %copy-done.6, bf16[1,2,256,256]{3,2,1,0:T(8,128)(2,1)S(1)} %copy-done, ...), custom_call_target="tpu_custom_call" | custom-call | tf_op jit(solution)/shard_map/pallas_call | solution.py:580
  64.8 0.6 copy.19
Async XLA Ops:
  2.6 0.7 copy-start.4
  2.6 0.7 copy-start.5
  2.6 0.7 copy-start.6
  3.3 0.9 %copy-start = (bf16[1,2,256,256]{3,2,1,0:T(8,128)(2,1)S(1)}, bf16[1,2,256,256]{3,2,1,0:T(8,128)(2,1)}, u32[]{:S(2)}) copy-start(bf16[1,2,256,256]{3,2,1,0:T(8,128)(2,1)} %image_hbm.1) | copy-start | bytes 786436
  4.2 0.8 %copy-start.1 = (s32[16,256,2]{1,2,0:T(2,128)S(1)}, s32[16,256,2]{1,2,0:T(2,128)}, u32[]{:S(2)}) copy-start(s32[16,256,2]{1,2,0:T(2,128)} %param.16) | copy-start | bytes 98308
  5.0 0.8 %copy-start.2 = (f32[16,256,2]{1,2,0:T(2,128)S(1)}, f32[16,256,2]{1,2,0:T(2,128)}, u32[]{:S(2)}) copy-start(f32[16,256,2]{1,2,0:T(2,128)} %param.17) | copy-start | bytes 98308
  5.7 0.7 %copy-start.3 = (bf16[16,2,256]{2,1,0:T(2,128)(2,1)S(1)}, bf16[16,2,256]{2,1,0:T(2,128)(2,1)}, u32[]{:S(2)}) copy-start(bf16[16,2,256]{2,1,0:T(2,128)(2,1)} %lines_hbm.1) | copy-start | bytes 49156

commit v3 on v2

--- a/solution.py
+++ b/solution.py
@@ -1,4 +1,3 @@
-import functools
 import math
 
 import jax
@@ -70,7 +69,6 @@
 
 
 def expect_kernel(
-    scale,
     class_hbm,
     precision_hbm,
     live_hbm,
@@ -103,8 +101,7 @@
     shifted,
     phases,
     squares,
-    product_high,
-    product_low,
+    products,
     turned,
     rows,
     sums,
@@ -185,47 +182,8 @@
     both = lines_ref[...]
     held[core, y_lo, z] = jnp.where(core == 0, both[:, 0, :], both[:, 1, :])
 
-    pl.semaphore_wait(barrier, len(peers))
-    for k in range(1, NX):
-        pl.semaphore_signal(ready, inc=1, device_id=along_x(k), device_id_type=MESH)
-    sent = []
-
-    def send_block(src, number, device):
-        copy = remote(src, src, gather_send.at[number], gather_recv.at[number], device)
-        copy.start()
-        sent.append(copy)
-        return copy
-
-    near_z = {
-        k: send_block(held.at[core, y_lo, z], k, along_z(k)) for k in (4, 3, 5, 2, 6, 1, 7)
-    }
-    far = 2 - 4 * core
-    steps = {1: 1, 2: far, 3: -1}
-    near_y = {}
-    swaps = []
-
-    def pass_along_y(k):
-        block = held.at[core, y_lo, (z + NZ - k) % NZ]
-        for d in (2, 1, 3):
-            near_y[d, k] = send_block(block, 8 * d + k, along_y(steps[d]))
-        swaps.append(send_block(block, 32 + k, sibling))
-
-    def pass_on(*distances):
-        for k in distances:
-            near_z[k].wait_recv()
-            pass_along_y(k)
-
-    def swap(*distances):
-        for k in distances:
-            for d, residue in ((1, y_lo + 3), (3, y_lo + 1), (2, y_lo + 2)):
-                near_y[d, k].wait_recv()
-                block = held.at[core, residue % Y_LO, (z + NZ - k) % NZ]
-                swaps.append(send_block(block, 32 + 8 * d + k, sibling))
-
-    pass_along_y(0)
     for load in loads[1:]:
         load.wait()
-
     alive = jnp.where(0 < live_ref[0], 1.0, 0.0).astype(F32)
     chosen = defocus_ref[class_ref[0]]
 
@@ -257,6 +215,44 @@
 
     lax.fori_loop(0, BOX // GROUP, shift_rows, 0)
 
+    pl.semaphore_wait(barrier, len(peers))
+    for k in range(1, NX):
+        pl.semaphore_signal(ready, inc=1, device_id=along_x(k), device_id_type=MESH)
+    sent = []
+
+    def send_block(src, number, device):
+        copy = remote(src, src, gather_send.at[number], gather_recv.at[number], device)
+        copy.start()
+        sent.append(copy)
+        return copy
+
+    near_z = {
+        k: send_block(held.at[core, y_lo, z], k, along_z(k)) for k in (4, 3, 5, 2, 6, 1, 7)
+    }
+    far = 2 - 4 * core
+    steps = {1: 1, 2: far, 3: -1}
+    near_y = {}
+    swaps = []
+
+    def pass_along_y(k):
+        block = held.at[core, y_lo, (z + NZ - k) % NZ]
+        for d in (2, 1, 3):
+            near_y[d, k] = send_block(block, 8 * d + k, along_y(steps[d]))
+        swaps.append(send_block(block, 32 + k, sibling))
+
+    def pass_on(*distances):
+        for k in distances:
+            near_z[k].wait_recv()
+            pass_along_y(k)
+
+    def swap(*distances):
+        for k in distances:
+            for d, residue in ((1, y_lo + 3), (3, y_lo + 1), (2, y_lo + 2)):
+                near_y[d, k].wait_recv()
+                block = held.at[core, residue % Y_LO, (z + NZ - k) % NZ]
+                swaps.append(send_block(block, 32 + 8 * d + k, sibling))
+
+    pass_along_y(0)
     lane = lax.broadcasted_iota(I32, (SHIFTS, ROWS), 1)
     freq = (lane >> 4) - BOX // 2
     part = (lane >> 3) & 1
@@ -381,48 +377,54 @@
     def diagonal(k, tile):
         return jnp.concatenate([tile, nothing] if k < GROUP // 2 else [nothing, tile], axis=1)
 
+    lane_pose = lax.broadcasted_iota(I32, (GROUP, 128), 1) < POSES
+
     def correlate(g, carry):
         at = pl.ds(pl.multiple_of(g * WIDE, WIDE), WIDE)
-        products = jnp.dot(shifted[at, :], slices[:, at], preferred_element_type=F32)
-        highs, lows = [], []
+        found = jnp.dot(shifted[at, :], slices[:, at], preferred_element_type=F32)
+        parts = []
         for k in range(GROUP):
             lane_at = k // (GROUP // 2) * 128
-            block = products[k * GROUP : (k + 1) * GROUP, lane_at : lane_at + 128]
-            block = jnp.where(lane_row == k % (GROUP // 2), block, 0.0)
+            block = found[k * GROUP : (k + 1) * GROUP, lane_at : lane_at + 128]
+            if k % (GROUP // 2):
+                block = pltpu.roll(block, 128 - k % (GROUP // 2) * POSES, 1)
+            block = jnp.where(lane_pose, block, 0.0)
             high = block.astype(BF16)
-            highs.append(diagonal(k, high))
-            lows.append(diagonal(k, (block - high.astype(F32)).astype(BF16)))
-        product_high[at, :] = jnp.concatenate(highs, axis=0)
-        product_low[at, :] = jnp.concatenate(lows, axis=0)
+            low = (block - high.astype(F32)).astype(BF16)
+            parts.append(jnp.concatenate([high, low], axis=1))
+        products[at, :] = jnp.concatenate(parts, axis=0)
         return carry
 
-    lax.fori_loop(0, BOX // GROUP, correlate, 0, unroll=4)
-    corr = jnp.dot(phases[...], product_high[...], preferred_element_type=F32)
-    corr = corr[: SHIFTS * SHIFTS] + corr[SHIFTS * SHIFTS :]
-    corr = corr + jnp.dot(
-        phases[: SHIFTS * SHIFTS, :], product_low[...], preferred_element_type=F32
-    )
-    corr = corr[:, : WIDE // 2] + corr[:, WIDE // 2 :]
-    for step in (64, 32, 16):
-        corr = corr + pltpu.roll(corr, step, 1)
+    lax.fori_loop(0, BOX // GROUP, correlate, 0, unroll=True)
+    corr = jnp.dot(phases[...], products[...], preferred_element_type=F32)
+    half = SHIFTS * SHIFTS
+    corr = corr[:half, :POSES] + (corr[half:, :POSES] + corr[:half, 128 : 128 + POSES])
     score = corr * (precision_ref[0] / BOX)
     top = jnp.max(score, axis=(0, 1), keepdims=True)
     terms = jnp.exp(score - top)
-    total = jnp.sum(terms, axis=(0, 1), keepdims=True) * (1.0 / 8.0)
+    total = jnp.sum(terms, axis=(0, 1), keepdims=True)
     posterior = terms / total
     loglik_ref[0] = ((top + jnp.log(total)) * alive)[0, 0]
-    posterior_t = posterior.T[:POSES]
+    posterior_t = posterior.T
     mass = jnp.sum(posterior_t, axis=1, keepdims=True)
 
     pairs = []
 
-    def spread_part(c):
-        columns = rows[:, c * BOX : (c + 1) * BOX]
-        pair_out[c] = jnp.dot(spread[KEEP:LINES, :], columns, preferred_element_type=F32).astype(BF16)
+    def spread_half(first_slot, c):
+        return jnp.dot(
+            spread[first_slot : first_slot + KEEP, :],
+            rows[:, c * BOX : (c + 1) * BOX],
+            preferred_element_type=F32,
+        )
+
+    def spread_other(c):
+        pair_out[c] = spread_half(KEEP, c).astype(BF16)
         copy = remote(pair_out.at[c], pair_in.at[c], pair_send.at[c], pair_recv.at[c], sibling)
         copy.start()
         pairs.append(copy)
-        sums[c] = jnp.dot(spread[:KEEP, :], columns, preferred_element_type=F32)
+
+    def spread_own(c):
+        sums[c] = spread_half(0, c)
 
     def square_rows(g, carry):
         at = pl.ds(pl.multiple_of(g * WIDE, WIDE), WIDE)
@@ -478,10 +480,11 @@
     ring8 = (4, 3, 5, 2, 6, 1, 7)
     ring4 = (2, 1, 3)
 
-    lax.fori_loop(0, BOX // GROUP, square_rows, 0, unroll=2)
-    spread_part(2)
+    lax.fori_loop(0, BOX // GROUP, square_rows, 0, unroll=4)
+    spread_other(2)
+    spread_own(2)
     turn_poses()
-    lax.fori_loop(0, BOX // GROUP, insert, 0, unroll=4)
+    lax.fori_loop(0, BOX // GROUP, insert, 0, unroll=True)
     pairs[0].wait_recv()
     c_sum = sums[2] + pair_in[2].astype(F32)
     for half in range(2):
@@ -495,8 +498,10 @@
     for k in ring8:
         cz_out[k] = c_rows(k).astype(BF16)
         c_hops.append(hop(k, cz_out.at[k], cz_in.at[k], along_z(k)))
-    spread_part(0)
-    spread_part(1)
+    spread_other(0)
+    spread_other(1)
+    spread_own(0)
+    spread_own(1)
 
     pairs[1].wait_recv()
     b_sum = (sums[0] + pair_in[0].astype(F32)).reshape(NX, NY, NZ, BOX)
@@ -515,11 +520,15 @@
 
     pl.semaphore_wait(ready, NX - 1)
 
-    def last(rows_out, rows_in, total, number, owner):
+    def last(rows_out, rows_in, total, number, size, owner):
         count = total.shape[0]
         rows_out[...] = total.reshape(count, 1, BOX)
         copies = []
-        for n in range(count - 1, 0, -1):
+        def hops_to(n):
+            far_step, near_step = divmod(n, 8)
+            return min(far_step, size - far_step) + min(near_step, 8 - near_step)
+
+        for n in sorted(range(1, count), key=hops_to, reverse=True):
             copies.append(
                 hop(number + n, rows_out.at[n], rows_in.at[n], owner(n))
             )
@@ -539,6 +548,7 @@
         c_last_in,
         c_sum,
         20,
+        NX,
         lambda n: device_at(z, (y + n % NY) % NY, (x + n // NY) % NX, core),
     )
     for k, copy in zip(ring4, a_hops):
@@ -549,6 +559,7 @@
         a_last_in,
         a_sum,
         52,
+        NY,
         lambda n: device_at((z + n % NZ) % NZ, (y + n // NZ) % NY, x, core),
     )
     for k, copy in zip(ring8, b_hops):
@@ -559,16 +570,17 @@
         b_last_in,
         b_sum,
         116,
+        NX,
         lambda n: device_at((z + n % NZ) % NZ, y, (x + n // NZ) % NX, core),
     )
-    out_ref[:, 2 * BOX :] = collect(c_last_in, c_sum, c_hops) * scale
-    out_ref[:, BOX : 2 * BOX] = collect(a_last_in, a_sum, a_hops) * scale
-    out_ref[:, :BOX] = collect(b_last_in, b_sum, b_hops) * scale
+    out_ref[:, 2 * BOX :] = collect(c_last_in, c_sum, c_hops)
+    out_ref[:, BOX : 2 * BOX] = collect(a_last_in, a_sum, a_hops)
+    out_ref[:, :BOX] = collect(b_last_in, b_sum, b_hops)
     for copy in sent + pairs + hops:
         copy.wait_send()
 
 
-def expect(scale, *operands):
+def expect(*operands):
     smem = pl.BlockSpec(memory_space=pltpu.SMEM)
     vmem = pl.BlockSpec(memory_space=pltpu.VMEM)
     dma = pltpu.SemaphoreType.DMA
@@ -578,7 +590,7 @@
         return [pltpu.VMEM(shape, kind), pltpu.VMEM(shape, kind)]
 
     return pl.pallas_call(
-        functools.partial(expect_kernel, scale),
+        expect_kernel,
         out_shape=(
             jax.ShapeDtypeStruct((1, 3 * BOX), F32),
             jax.ShapeDtypeStruct((1,), F32),
@@ -600,7 +612,6 @@
             pltpu.VMEM((ROWS, 2 * BOX), BF16),
             pltpu.VMEM((2 * SHIFTS * SHIFTS, ROWS), BF16),
             pltpu.VMEM((BOX, BOX), F32),
-            pltpu.VMEM((ROWS, WIDE), BF16),
             pltpu.VMEM((ROWS, WIDE), BF16),
             pltpu.VMEM((POSES, ROWS), BF16),
             pltpu.VMEM((ROWS, 3 * BOX), BF16),
@@ -624,7 +635,7 @@
             pltpu.SemaphoreType.REGULAR,
         ],
         compiler_params=pltpu.CompilerParams(
-            collective_id=0, has_side_effects=True, vmem_limit_bytes=48 * 1024 * 1024
+            collective_id=0, has_side_effects=True, vmem_limit_bytes=60 * 1024 * 1024
         ),
     )(*operands)
 
@@ -645,7 +656,6 @@
     weight = jnp.transpose(line_weight, (0, 2, 1))
     particle_total = particles.shape[0] * lax.axis_size("slab") * lax.axis_size("grp")
     owned, loglik = expect(
-        LINES / (POSES * particle_total),
         defocus_class,
         noise_precision,
         live_count,
@@ -657,7 +667,7 @@
         weight,
         reference_lines,
     )
-    return owned.reshape(1, 3, BOX), loglik
+    return owned.reshape(1, 3, BOX) * (LINES / (POSES * particle_total)), loglik
 
 
 def solution(mesh):

time: 67.4 us -> 62 us (0.920)
  local copies, waits for them, and re-layouts: 4.42 us -> 0.65 us
  Pallas kernels: 58.3 us -> 56.1 us
    unnamed x15 -> x2, local copies, waits for them, and re-layouts: 4.42 us -> 0.65 us
    pallas_call x1, Pallas kernels: 58.3 us -> 56.1 us  [expect(): pl.pallas_call(expect_kernel, out_shape=(jax.ShapeDtypeStruct((1, 3 * BOX...]
where the time goes in v3:
time: 62 us; the launch traced here: 61.7 us
  Pallas kernels  56.1 us (90%)
  between operations  4.35 us (7%)
  local copies, waits for them, and re-layouts  0.65 us (1%)
    pallas_call x1, Pallas kernels, expect(): pl.pallas_call(expect_kernel, out_shape=(jax.ShapeDtypeStruct((1, 3 * BOX...  56.1 us

profile of v3, /device:TPU:1, one launch (start us, length us, event | category | flops | bytes accessed | tf_op | source)
XLA Modules:
  0.0 61.7 jit_solution(6104683841007647228)
XLA Ops:
  2.6 56.1 %shard_map.113 = (f32[1,768]{1,0:T(1,128)}, f32[1]{0:T(128)}) custom-call(s32[1]{0:T(128)S(6)} %copy.15.class_hbm, f32[1]{0:T(128)S(6)} %copy.16.precision_hbm, s32[1]{0:T(128)S(6)} %copy.17.live_hbm, f32[16]{0:T(128)} %defocus_hbm.1, s32[8]{0:T(128)} %row_shift_hbm.1, s32[8]{0:T(128)} %column_shift_hbm.1, bf16[1,2,256,256]{3,2,1,0:T(8,128)(2,1)} %image_hbm.1, ...), custom_call_target="tpu_custom_call" | custom-call | tf_op jit(solution)/shard_map/pallas_call | solution.py:592
  58.7 0.0 copy-start
  58.7 0.7 %copy-done = f32[1,768]{1,0:T(1,128)S(1)} copy-done((f32[1,768]{1,0:T(1,128)S(1)}, f32[1,768]{1,0:T(1,128)}, u32[]{:S(2)}) %copy-start) | copy-done | bytes 3096
  59.4 0.6 broadcast_multiply_fusion
Async XLA Ops:
  58.7 0.7 %copy-start = (f32[1,768]{1,0:T(1,128)S(1)}, f32[1,768]{1,0:T(1,128)}, u32[]{:S(2)}) copy-start(f32[1,768]{1,0:T(1,128)} %get-tuple-element.4) | copy-start | bytes 9220

commit v4 on v3

--- a/solution.py
+++ b/solution.py
@@ -12,6 +12,7 @@
 F32 = jnp.float32
 BF16 = jnp.bfloat16
 I32 = jnp.int32
+I16 = jnp.int16
 
 NX, NY, NZ, Y_LO = 4, 8, 8, 4
 SLABS = NZ * Y_LO
@@ -126,6 +127,8 @@
     pair_recv,
     hop_send,
     hop_recv,
+    last_send,
+    last_recv,
     ready,
 ):
     loads = [
@@ -218,39 +221,42 @@
     pl.semaphore_wait(barrier, len(peers))
     for k in range(1, NX):
         pl.semaphore_signal(ready, inc=1, device_id=along_x(k), device_id_type=MESH)
-    sent = []
-
-    def send_block(src, number, device):
-        copy = remote(src, src, gather_send.at[number], gather_recv.at[number], device)
+
+    def send_block(src, send, recv, device):
+        copy = remote(src, src, gather_send.at[send], gather_recv.at[recv], device)
         copy.start()
-        sent.append(copy)
         return copy
 
+    def landed(blocks, number):
+        pltpu.make_async_copy(blocks, blocks, gather_recv.at[number]).wait()
+
+    def left(blocks, number):
+        pltpu.make_async_copy(blocks, blocks, gather_send.at[number]).wait()
+
+    groups = ((0, 1, 7), (2, 6), (3, 5, 4))
     near_z = {
-        k: send_block(held.at[core, y_lo, z], k, along_z(k)) for k in (4, 3, 5, 2, 6, 1, 7)
+        k: send_block(held.at[core, y_lo, z], 0, k, along_z(k)) for k in (4, 3, 5, 2, 6, 1, 7)
     }
     far = 2 - 4 * core
     steps = {1: 1, 2: far, 3: -1}
-    near_y = {}
-    swaps = []
 
     def pass_along_y(k):
         block = held.at[core, y_lo, (z + NZ - k) % NZ]
+        group = [k in members for members in groups].index(True)
         for d in (2, 1, 3):
-            near_y[d, k] = send_block(block, 8 * d + k, along_y(steps[d]))
-        swaps.append(send_block(block, 32 + k, sibling))
+            send_block(block, 1, NZ + group, along_y(steps[d]))
+        send_block(block, 2, 11, sibling)
 
     def pass_on(*distances):
         for k in distances:
             near_z[k].wait_recv()
             pass_along_y(k)
 
-    def swap(*distances):
-        for k in distances:
-            for d, residue in ((1, y_lo + 3), (3, y_lo + 1), (2, y_lo + 2)):
-                near_y[d, k].wait_recv()
-                block = held.at[core, residue % Y_LO, (z + NZ - k) % NZ]
-                swaps.append(send_block(block, 32 + 8 * d + k, sibling))
+    def swap(group):
+        landed(held.at[core, pl.ds(0, 3), pl.ds(0, len(groups[group]))], NZ + group)
+        for k in groups[group]:
+            for residue in (y_lo + 3, y_lo + 1, y_lo + 2):
+                send_block(held.at[core, residue % Y_LO, (z + NZ - k) % NZ], 2, 11, sibling)
 
     pass_along_y(0)
     lane = lax.broadcasted_iota(I32, (SHIFTS, ROWS), 1)
@@ -307,34 +313,40 @@
             )
             for n in range(8)
         ]
-        slots[0:1, at] = (found[0] * 16.0 + found[1]).astype(I32)
-        slots[1:2, at] = (found[2] * 16.0 + found[3]).astype(I32)
+        for n in range(2):
+            slot = (found[2 * n] * 16.0 + found[2 * n + 1]).astype(I32)
+            slots[n, :, at] = jnp.broadcast_to(slot, (GROUP, WIDE)).astype(I16)
         for n in range(4):
-            weights[n : n + 1, at] = found[4 + n]
+            weights[n, :, at] = jnp.broadcast_to(found[4 + n], (GROUP, WIDE)).astype(BF16)
         return carry
 
     lax.fori_loop(0, 8, table_rows, 0, unroll=2)
     pass_on(2, 6)
     lax.fori_loop(8, BOX // GROUP, table_rows, 0, unroll=2)
     pass_on(3, 5, 4)
-    slot_row = lax.broadcasted_iota(I32, (LINES, WIDE), 0)
+    slot_row = lax.broadcasted_iota(I32, (GROUP, WIDE), 0).astype(I16)
 
     def spread_rows(g, carry):
         at = pl.ds(pl.multiple_of(g * WIDE, WIDE), WIDE)
-        is_first = slot_row == slots[0:1, at]
-        is_second = slot_row == slots[1:2, at]
-        high = jnp.where(is_first, weights[0:1, at], jnp.where(is_second, weights[1:2, at], 0.0))
-        low = jnp.where(is_first, weights[2:3, at], jnp.where(is_second, weights[3:4, at], 0.0))
-        spread[:LINES, at] = high.astype(BF16)
-        spread[LINES:, at] = low.astype(BF16)
+        first_slot, second_slot = slots[0, :, at], slots[1, :, at]
+        parts = [weights[n, :, at] for n in range(4)]
+        for block in range(LINES // GROUP):
+            row = slot_row + jnp.int16(block * GROUP)
+            is_first = first_slot == row
+            is_second = second_slot == row
+            for n, base in ((0, 0), (2, LINES)):
+                rest = jnp.where(is_second, parts[n + 1], jnp.zeros_like(parts[n]))
+                spread[base + block * GROUP : base + (block + 1) * GROUP, at] = jnp.where(
+                    is_first, parts[n], rest
+                )
         return carry
 
     lax.fori_loop(0, 5, spread_rows, 0)
-    swap(0, 1, 7)
+    swap(0)
     lax.fori_loop(5, 10, spread_rows, 0)
-    swap(2, 6)
+    swap(1)
     lax.fori_loop(10, BOX // GROUP, spread_rows, 0)
-    swap(3, 5, 4)
+    swap(2)
 
     slot_rows = held_row(lax.broadcasted_iota(I32, (1, LINES), 1), z, y, x, core)
     order = jnp.where(
@@ -366,8 +378,7 @@
 
     transpose_half(core)
     slice_half(core)
-    for copy in swaps:
-        copy.wait_recv()
+    landed(held.at[1 - core], 11)
     transpose_half(1 - core)
     slice_half(1 - core)
 
@@ -519,72 +530,81 @@
     a_sum = a_sum[0]
 
     pl.semaphore_wait(ready, NX - 1)
+    left(held.at[core, y_lo, pl.ds(0, NZ - 1)], 0)
+    left(held.at[core, pl.ds(0, 3)], 1)
+    left(held.at[core], 2)
+    for copy in pairs + hops:
+        copy.wait_send()
 
     def last(rows_out, rows_in, total, number, size, owner):
         count = total.shape[0]
         rows_out[...] = total.reshape(count, 1, BOX)
-        copies = []
+
         def hops_to(n):
             far_step, near_step = divmod(n, 8)
             return min(far_step, size - far_step) + min(near_step, 8 - near_step)
 
         for n in sorted(range(1, count), key=hops_to, reverse=True):
-            copies.append(
-                hop(number + n, rows_out.at[n], rows_in.at[n], owner(n))
-            )
-        return copies
-
-    def collect(rows_in, total, copies):
-        for copy in copies:
-            copy.wait_recv()
+            remote(
+                rows_out.at[n], rows_in.at[n], last_send.at[number], last_recv.at[number], owner(n)
+            ).start()
+
+    def collect(rows_in, total, number):
+        arrived = rows_in.at[pl.ds(1, total.shape[0] - 1)]
+        pltpu.make_async_copy(arrived, arrived, last_recv.at[number]).wait()
         return total[0:1, :] + jnp.sum(rows_in[1:], axis=0)
+
+    def drain(rows_out, number):
+        gone = rows_out.at[pl.ds(1, rows_out.shape[0] - 1)]
+        pltpu.make_async_copy(gone, gone, last_send.at[number]).wait()
 
     c_sum = c_rows(0)
     for k, copy in zip(ring8, c_hops):
         copy.wait_recv()
         c_sum = c_sum + cz_in[k].astype(F32)
-    c_hops = last(
+    last(
         c_last_out,
         c_last_in,
         c_sum,
-        20,
+        2,
         NX,
         lambda n: device_at(z, (y + n % NY) % NY, (x + n // NY) % NX, core),
     )
     for k, copy in zip(ring4, a_hops):
         copy.wait_recv()
         a_sum = a_sum + ax_in[k].astype(F32)
-    a_hops = last(
+    last(
         a_last_out,
         a_last_in,
         a_sum,
-        52,
+        1,
         NY,
         lambda n: device_at((z + n % NZ) % NZ, (y + n // NZ) % NY, x, core),
     )
     for k, copy in zip(ring8, b_hops):
         copy.wait_recv()
         b_sum = b_sum + by_in[k].astype(F32)
-    b_hops = last(
+    last(
         b_last_out,
         b_last_in,
         b_sum,
-        116,
+        0,
         NX,
         lambda n: device_at((z + n % NZ) % NZ, y, (x + n // NZ) % NX, core),
     )
-    out_ref[:, 2 * BOX :] = collect(c_last_in, c_sum, c_hops)
-    out_ref[:, BOX : 2 * BOX] = collect(a_last_in, a_sum, a_hops)
-    out_ref[:, :BOX] = collect(b_last_in, b_sum, b_hops)
-    for copy in sent + pairs + hops:
-        copy.wait_send()
+    out_ref[:, 2 * BOX :] = collect(c_last_in, c_sum, 2)
+    out_ref[:, BOX : 2 * BOX] = collect(a_last_in, a_sum, 1)
+    out_ref[:, :BOX] = collect(b_last_in, b_sum, 0)
+    drain(c_last_out, 2)
+    drain(a_last_out, 1)
+    drain(b_last_out, 0)
 
 
 def expect(*operands):
     smem = pl.BlockSpec(memory_space=pltpu.SMEM)
     vmem = pl.BlockSpec(memory_space=pltpu.VMEM)
     dma = pltpu.SemaphoreType.DMA
-    hop_count = 116 + NX * NZ
+    hop_count = 2 * NZ + NX
 
     def both_ways(shape, kind):
         return [pltpu.VMEM(shape, kind), pltpu.VMEM(shape, kind)]
@@ -604,8 +624,8 @@
         + [dma((10,))]
         + [
             pltpu.VMEM((2, Y_LO, NZ, 16, BOX), BF16),
-            pltpu.VMEM((2, ROWS), I32),
-            pltpu.VMEM((4, ROWS), F32),
+            pltpu.VMEM((2, GROUP, ROWS), I16),
+            pltpu.VMEM((4, GROUP, ROWS), BF16),
             pltpu.VMEM((2 * BOX, 2 * LINES), BF16),
             pltpu.VMEM((2 * LINES, ROWS), BF16),
             pltpu.VMEM((2 * BOX, ROWS), BF16),
@@ -626,12 +646,14 @@
         + both_ways((NX * NZ, 1, BOX), F32)
         + both_ways((NX * NY, 1, BOX), F32)
         + [
-            dma((2 * SLABS,)),
-            dma((2 * SLABS,)),
+            dma((3,)),
+            dma((12,)),
             dma((3,)),
             dma((3,)),
             dma((hop_count,)),
             dma((hop_count,)),
+            dma((3,)),
+            dma((3,)),
             pltpu.SemaphoreType.REGULAR,
         ],
         compiler_params=pltpu.CompilerParams(

time: 62 us -> 57.4 us (0.926)
  the two profiles are of different devices: /device:TPU:1 before, /device:TPU:8 now
where the time goes in v4:
time: 57.4 us; the launch traced here: 57.1 us
  Pallas kernels  51.5 us (90%)
  between operations  4.35 us (8%)
  local copies, waits for them, and re-layouts  0.65 us (1%)
  other arithmetic  0.58 us (1%)
    pallas_call x1, Pallas kernels, expect(): pl.pallas_call(expect_kernel, out_shape=(jax.ShapeDtypeStruct((1, 3 * BOX...  51.5 us

profile of v4, /device:TPU:8, one launch (start us, length us, event | category | flops | bytes accessed | tf_op | source)
XLA Modules:
  0.0 57.1 jit_solution(14938182062471807877)
XLA Ops:
  2.6 51.5 %shard_map.113 = (f32[1,768]{1,0:T(1,128)}, f32[1]{0:T(128)}) custom-call(s32[1]{0:T(128)S(6)} %copy.15.class_hbm, f32[1]{0:T(128)S(6)} %copy.16.precision_hbm, s32[1]{0:T(128)S(6)} %copy.17.live_hbm, f32[16]{0:T(128)} %defocus_hbm.1, s32[8]{0:T(128)} %row_shift_hbm.1, s32[8]{0:T(128)} %column_shift_hbm.1, bf16[1,2,256,256]{3,2,1,0:T(8,128)(2,1)} %image_hbm.1, ...), custom_call_target="tpu_custom_call" | custom-call | tf_op jit(solution)/shard_map/pallas_call | solution.py:612
  54.1 0.0 copy-start
  54.1 0.7 %copy-done = f32[1,768]{1,0:T(1,128)S(1)} copy-done((f32[1,768]{1,0:T(1,128)S(1)}, f32[1,768]{1,0:T(1,128)}, u32[]{:S(2)}) %copy-start) | copy-done | bytes 3096
  54.8 0.6 %broadcast_multiply_fusion = f32[1,768]{1,0:T(1,128)} fusion(f32[1,768]{1,0:T(1,128)S(1)} %copy-done), kind=kLoop, calls=%fused_computation | loop fusion | flops 768 | bytes 6144 | tf_op jit(solution)/shard_map/mul | solution.py:692
Async XLA Ops:
  54.1 0.7 %copy-start = (f32[1,768]{1,0:T(1,128)S(1)}, f32[1,768]{1,0:T(1,128)}, u32[]{:S(2)}) copy-start(f32[1,768]{1,0:T(1,128)} %get-tuple-element.4) | copy-start | bytes 9220

commit v5 on v4

--- a/solution.py
+++ b/solution.py
@@ -105,6 +105,9 @@
     products,
     turned,
     rows,
+    pose_slots,
+    pose_weights,
+    spread_square,
     sums,
     strided,
     pair_out,
@@ -131,6 +134,37 @@
     last_recv,
     ready,
 ):
+    z, y, x, core = place()
+    y_lo = y % Y_LO
+    sibling = device_at(z, y, x, 1 - core)
+
+    def along_x(k):
+        return device_at(z, y, (x + k) % NX, core)
+
+    def along_y(k):
+        return device_at(z, (y + NY + k) % NY, x, core)
+
+    def along_z(k):
+        return device_at((z + k) % NZ, y, x, core)
+
+    def remote(src, dst, send, recv, device):
+        return pltpu.make_async_remote_copy(
+            src_ref=src,
+            dst_ref=dst,
+            send_sem=send,
+            recv_sem=recv,
+            device_id=device,
+            device_id_type=MESH,
+        )
+
+    barrier = pltpu.get_barrier_semaphore()
+    peers = [sibling]
+    peers += [along_x(k) for k in range(1, NX)]
+    peers += [along_y(k) for k in range(1, NY)]
+    peers += [along_z(k) for k in range(1, NZ)]
+    for peer in peers:
+        pl.semaphore_signal(barrier, inc=1, device_id=peer, device_id_type=MESH)
+
     loads = [
         pltpu.make_async_copy(src, dst, load_sem.at[n])
         for n, (src, dst) in enumerate(
@@ -150,36 +184,6 @@
     ]
     for load in loads:
         load.start()
-    z, y, x, core = place()
-    y_lo = y % Y_LO
-    sibling = device_at(z, y, x, 1 - core)
-
-    def along_x(k):
-        return device_at(z, y, (x + k) % NX, core)
-
-    def along_y(k):
-        return device_at(z, (y + NY + k) % NY, x, core)
-
-    def along_z(k):
-        return device_at((z + k) % NZ, y, x, core)
-
-    def remote(src, dst, send, recv, device):
-        return pltpu.make_async_remote_copy(
-            src_ref=src,
-            dst_ref=dst,
-            send_sem=send,
-            recv_sem=recv,
-            device_id=device,
-            device_id_type=MESH,
-        )
-
-    barrier = pltpu.get_barrier_semaphore()
-    peers = [sibling]
-    peers += [along_x(k) for k in range(1, NX)]
-    peers += [along_y(k) for k in range(1, NY)]
-    peers += [along_z(k) for k in range(1, NZ)]
-    for peer in peers:
-        pl.semaphore_signal(barrier, inc=1, device_id=peer, device_id_type=MESH)
 
     loads[0].wait()
     both = lines_ref[...]
@@ -346,11 +350,40 @@
     lax.fori_loop(5, 10, spread_rows, 0)
     swap(1)
     lax.fori_loop(10, BOX // GROUP, spread_rows, 0)
+
+    square = squares[...].astype(BF16)
+    slot_rows = lax.broadcasted_iota(I32, (GROUP, BOX), 0).astype(I16)
+    for n, table, target, kind in (
+        (0, first, pose_slots, I16),
+        (1, second, pose_slots, I16),
+        (0, first_high, pose_weights, BF16),
+        (1, second_high, pose_weights, BF16),
+    ):
+        for p in range(POSES):
+            target[n, p * GROUP : (p + 1) * GROUP, :] = jnp.broadcast_to(
+                table[p : p + 1, :], (GROUP, BOX)
+            ).astype(kind)
+
+    def spread_squares(p, carry):
+        rows_p = pl.ds(pl.multiple_of(p * GROUP, GROUP), GROUP)
+        first_slot, second_slot = pose_slots[0, rows_p, :], pose_slots[1, rows_p, :]
+        first_part, second_part = pose_weights[0, rows_p, :], pose_weights[1, rows_p, :]
+        blocks = []
+        for block in range(LINES // GROUP):
+            row = slot_rows + jnp.int16(block * GROUP)
+            rest = jnp.where(second_slot == row, second_part, jnp.zeros_like(second_part))
+            blocks.append(jnp.where(first_slot == row, first_part, rest))
+        spread_square[p] = jnp.dot(
+            jnp.concatenate(blocks, axis=0), square, preferred_element_type=F32
+        )
+        return carry
+
+    lax.fori_loop(0, POSES, spread_squares, 0, unroll=4)
     swap(2)
 
-    slot_rows = held_row(lax.broadcasted_iota(I32, (1, LINES), 1), z, y, x, core)
+    slot_lines = held_row(lax.broadcasted_iota(I32, (1, LINES), 1), z, y, x, core)
     order = jnp.where(
-        lax.broadcasted_iota(I32, (LINES, LINES), 0) == slot_rows, 1.0, 0.0
+        lax.broadcasted_iota(I32, (LINES, LINES), 0) == slot_lines, 1.0, 0.0
     ).astype(BF16)
 
     def transpose_half(c):
@@ -419,6 +452,8 @@
     posterior_t = posterior.T
     mass = jnp.sum(posterior_t, axis=1, keepdims=True)
 
+    ring8 = (4, 3, 5, 2, 6, 1, 7)
+    ring4 = (2, 1, 3)
     pairs = []
 
     def spread_half(first_slot, c):
@@ -428,22 +463,38 @@
             preferred_element_type=F32,
         )
 
-    def spread_other(c):
-        pair_out[c] = spread_half(KEEP, c).astype(BF16)
+    def send_pair(c, total):
+        pair_out[c] = total.astype(BF16)
         copy = remote(pair_out.at[c], pair_in.at[c], pair_send.at[c], pair_recv.at[c], sibling)
         copy.start()
         pairs.append(copy)
 
+    part = NY * NZ
+    a_pairs = {}
+
+    def send_pair_blocks(c, total):
+        pair_out[c] = total.astype(BF16)
+        for n, k in enumerate(ring4 + (0,)):
+            block = pl.ds(k * part, part)
+            copy = remote(
+                pair_out.at[c, block],
+                pair_in.at[c, block],
+                pair_send.at[3 + n],
+                pair_recv.at[3 + n],
+                sibling,
+            )
+            copy.start()
+            pairs.append(copy)
+            a_pairs[k] = copy
+
     def spread_own(c):
         sums[c] = spread_half(0, c)
 
-    def square_rows(g, carry):
-        at = pl.ds(pl.multiple_of(g * WIDE, WIDE), WIDE)
-        square = squares[pl.ds(pl.multiple_of(g * GROUP, GROUP), GROUP), :]
-        rows[at, 2 * BOX :] = jnp.concatenate(
-            [square[k : k + 1, :] * mass for k in range(GROUP)], axis=0
-        ).astype(BF16)
-        return carry
+    def spread_mass(first_slot):
+        total = spread_square[0, first_slot : first_slot + KEEP, :] * mass[0:1, :]
+        for p in range(1, POSES):
+            total = total + spread_square[p, first_slot : first_slot + KEEP, :] * mass[p : p + 1, :]
+        return total
 
     def turn_poses():
         high = posterior_t.astype(BF16)
@@ -475,7 +526,7 @@
             ],
             axis=0,
         )
-        rows[at, : 2 * BOX] = jnp.dot(
+        rows[at, :] = jnp.dot(
             weight, shifted[at, :], preferred_element_type=F32
         ).astype(BF16)
         return carry
@@ -488,12 +539,9 @@
         hops.append(copy)
         return copy
 
-    ring8 = (4, 3, 5, 2, 6, 1, 7)
-    ring4 = (2, 1, 3)
-
-    lax.fori_loop(0, BOX // GROUP, square_rows, 0, unroll=4)
-    spread_other(2)
-    spread_own(2)
+
+    send_pair(2, spread_mass(KEEP))
+    sums[2] = spread_mass(0)
     turn_poses()
     lax.fori_loop(0, BOX // GROUP, insert, 0, unroll=True)
     pairs[0].wait_recv()
@@ -509,8 +557,8 @@
     for k in ring8:
         cz_out[k] = c_rows(k).astype(BF16)
         c_hops.append(hop(k, cz_out.at[k], cz_in.at[k], along_z(k)))
-    spread_other(0)
-    spread_other(1)
+    send_pair(0, spread_half(KEEP, 0))
+    send_pair_blocks(1, spread_half(KEEP, 1))
     spread_own(0)
     spread_own(1)
 
@@ -521,13 +569,16 @@
         by_out[k] = b_sum[:, k].reshape(NX * NZ, BOX).astype(BF16)
         b_hops.append(hop(NZ + k, by_out.at[k], by_in.at[k], along_y(k)))
     b_sum = b_sum[:, 0].reshape(NX * NZ, BOX)
-    pairs[2].wait_recv()
-    a_sum = (sums[1] + pair_in[1].astype(F32)).reshape(NX, NY * NZ, BOX)
+    def a_block(k):
+        a_pairs[k].wait_recv()
+        block = pl.ds(k * part, part)
+        return sums[1, block, :] + pair_in[1, block, :].astype(F32)
+
     a_hops = []
     for k in ring4:
-        ax_out[k] = a_sum[k].astype(BF16)
+        ax_out[k] = a_block(k).astype(BF16)
         a_hops.append(hop(2 * NZ + k, ax_out.at[k], ax_in.at[k], along_x(k)))
-    a_sum = a_sum[0]
+    a_sum = a_block(0)
 
     pl.semaphore_wait(ready, NX - 1)
     left(held.at[core, y_lo, pl.ds(0, NZ - 1)], 0)
@@ -634,7 +685,10 @@
             pltpu.VMEM((BOX, BOX), F32),
             pltpu.VMEM((ROWS, WIDE), BF16),
             pltpu.VMEM((POSES, ROWS), BF16),
-            pltpu.VMEM((ROWS, 3 * BOX), BF16),
+            pltpu.VMEM((ROWS, 2 * BOX), BF16),
+            pltpu.VMEM((2, POSES * GROUP, BOX), I16),
+            pltpu.VMEM((2, POSES * GROUP, BOX), BF16),
+            pltpu.VMEM((POSES, LINES, BOX), F32),
             pltpu.VMEM((3, KEEP, BOX), F32),
             pltpu.VMEM((2, KEEP, BOX // 2), F32),
         ]
@@ -648,8 +702,8 @@
         + [
             dma((3,)),
             dma((12,)),
-            dma((3,)),
-            dma((3,)),
+            dma((7,)),
+            dma((7,)),
             dma((hop_count,)),
             dma((hop_count,)),
             dma((3,)),

time: 57.4 us -> 57.4 us (level)
  no operation moved by 1% of the time
where the time goes in v5:
time: 57.4 us; the launch traced here: 57.1 us
  Pallas kernels  51.5 us (90%)
  between operations  4.35 us (8%)
  local copies, waits for them, and re-layouts  0.65 us (1%)
  other arithmetic  0.58 us (1%)
    pallas_call x1, Pallas kernels, expect(): pl.pallas_call(expect_kernel, out_shape=(jax.ShapeDtypeStruct((1, 3 * BOX...  51.5 us

profile of v5, /device:TPU:8, one launch (start us, length us, event | category | flops | bytes accessed | tf_op | source)
XLA Modules:
  0.0 57.1 jit_solution(5558889034126405650)
XLA Ops:
  2.6 51.5 %shard_map.113 = (f32[1,768]{1,0:T(1,128)}, f32[1]{0:T(128)}) custom-call(s32[1]{0:T(128)S(6)} %copy.15.class_hbm, f32[1]{0:T(128)S(6)} %copy.16.precision_hbm, s32[1]{0:T(128)S(6)} %copy.17.live_hbm, f32[16]{0:T(128)} %defocus_hbm.1, s32[8]{0:T(128)} %row_shift_hbm.1, s32[8]{0:T(128)} %column_shift_hbm.1, bf16[1,2,256,256]{3,2,1,0:T(8,128)(2,1)} %image_hbm.1, ...), custom_call_target="tpu_custom_call" | custom-call | tf_op jit(solution)/shard_map/pallas_call | solution.py:663
  54.1 0.0 copy-start
  54.1 0.7 %copy-done = f32[1,768]{1,0:T(1,128)S(1)} copy-done((f32[1,768]{1,0:T(1,128)S(1)}, f32[1,768]{1,0:T(1,128)}, u32[]{:S(2)}) %copy-start) | copy-done | bytes 3096
  54.7 0.6 %broadcast_multiply_fusion = f32[1,768]{1,0:T(1,128)} fusion(f32[1,768]{1,0:T(1,128)S(1)} %copy-done), kind=kLoop, calls=%fused_computation | loop fusion | flops 768 | bytes 6144 | tf_op jit(solution)/shard_map/mul | solution.py:746
Async XLA Ops:
  54.1 0.7 %copy-start = (f32[1,768]{1,0:T(1,128)S(1)}, f32[1,768]{1,0:T(1,128)}, u32[]{:S(2)}) copy-start(f32[1,768]{1,0:T(1,128)} %get-tuple-element.4) | copy-start | bytes 9220

commit v6 on v5

--- a/solution.py
+++ b/solution.py
@@ -189,6 +189,47 @@
     both = lines_ref[...]
     held[core, y_lo, z] = jnp.where(core == 0, both[:, 0, :], both[:, 1, :])
 
+    pl.semaphore_wait(barrier, len(peers))
+    for k in range(1, NX):
+        pl.semaphore_signal(ready, inc=1, device_id=along_x(k), device_id_type=MESH)
+
+    def send_block(src, send, recv, device):
+        copy = remote(src, src, gather_send.at[send], gather_recv.at[recv], device)
+        copy.start()
+        return copy
+
+    def landed(blocks, number):
+        pltpu.make_async_copy(blocks, blocks, gather_recv.at[number]).wait()
+
+    def left(blocks, number):
+        pltpu.make_async_copy(blocks, blocks, gather_send.at[number]).wait()
+
+    groups = ((0, 1, 7), (2, 6), (3, 5, 4))
+    near_z = {
+        k: send_block(held.at[core, y_lo, z], 0, k, along_z(k)) for k in (4, 3, 5, 2, 6, 1, 7)
+    }
+    far = 2 - 4 * core
+    steps = {1: 1, 2: far, 3: -1}
+
+    def pass_along_y(k):
+        block = held.at[core, y_lo, (z + NZ - k) % NZ]
+        group = [k in members for members in groups].index(True)
+        for d in (2, 1, 3):
+            send_block(block, 1, NZ + group, along_y(steps[d]))
+        send_block(block, 2, 11, sibling)
+
+    def pass_on(*distances):
+        for k in distances:
+            near_z[k].wait_recv()
+            pass_along_y(k)
+
+    def swap(group):
+        landed(held.at[core, pl.ds(0, 3), pl.ds(0, len(groups[group]))], NZ + group)
+        for k in groups[group]:
+            for residue in (y_lo + 3, y_lo + 1, y_lo + 2):
+                send_block(held.at[core, residue % Y_LO, (z + NZ - k) % NZ], 2, 11, sibling)
+
+    pass_along_y(0)
     for load in loads[1:]:
         load.wait()
     alive = jnp.where(0 < live_ref[0], 1.0, 0.0).astype(F32)
@@ -206,7 +247,7 @@
         kx = pl.ds(pl.multiple_of(g * GROUP, GROUP), GROUP)
         freq_x = (row_in_group + (g * GROUP - BOX // 2)).astype(F32) / BOX
         ctf = -jnp.sin(chosen * (freq_x * freq_x + freq_y * freq_y) + 0.1) * alive
-        squares[kx, :] = ctf * ctf
+        squares[kx, :] = (ctf * ctf).astype(BF16)
         real = ctf * image_ref[0, 0, kx, :].astype(F32)
         imag = ctf * image_ref[0, 1, kx, :].astype(F32)
         blocks = []
@@ -220,49 +261,7 @@
         shifted[at, :] = jnp.concatenate(blocks, axis=0).astype(BF16)
         return carry
 
-    lax.fori_loop(0, BOX // GROUP, shift_rows, 0)
-
-    pl.semaphore_wait(barrier, len(peers))
-    for k in range(1, NX):
-        pl.semaphore_signal(ready, inc=1, device_id=along_x(k), device_id_type=MESH)
-
-    def send_block(src, send, recv, device):
-        copy = remote(src, src, gather_send.at[send], gather_recv.at[recv], device)
-        copy.start()
-        return copy
-
-    def landed(blocks, number):
-        pltpu.make_async_copy(blocks, blocks, gather_recv.at[number]).wait()
-
-    def left(blocks, number):
-        pltpu.make_async_copy(blocks, blocks, gather_send.at[number]).wait()
-
-    groups = ((0, 1, 7), (2, 6), (3, 5, 4))
-    near_z = {
-        k: send_block(held.at[core, y_lo, z], 0, k, along_z(k)) for k in (4, 3, 5, 2, 6, 1, 7)
-    }
-    far = 2 - 4 * core
-    steps = {1: 1, 2: far, 3: -1}
-
-    def pass_along_y(k):
-        block = held.at[core, y_lo, (z + NZ - k) % NZ]
-        group = [k in members for members in groups].index(True)
-        for d in (2, 1, 3):
-            send_block(block, 1, NZ + group, along_y(steps[d]))
-        send_block(block, 2, 11, sibling)
-
-    def pass_on(*distances):
-        for k in distances:
-            near_z[k].wait_recv()
-            pass_along_y(k)
-
-    def swap(group):
-        landed(held.at[core, pl.ds(0, 3), pl.ds(0, len(groups[group]))], NZ + group)
-        for k in groups[group]:
-            for residue in (y_lo + 3, y_lo + 1, y_lo + 2):
-                send_block(held.at[core, residue % Y_LO, (z + NZ - k) % NZ], 2, 11, sibling)
-
-    pass_along_y(0)
+
     lane = lax.broadcasted_iota(I32, (SHIFTS, ROWS), 1)
     freq = (lane >> 4) - BOX // 2
     part = (lane >> 3) & 1
@@ -276,7 +275,6 @@
                 [jnp.where((lane & 7) == t + u, table, 0.0) for u in range(2)], axis=0
             ).astype(BF16)
 
-    pass_on(1, 7)
     first = slot_of(index_ref[:, 0, :], z, y, x, core)
     second = slot_of(index_ref[:, 1, :], z, y, x, core)
     first_weight = weight_ref[:, 0, :]
@@ -299,15 +297,19 @@
         ],
         axis=0,
     ).astype(BF16)
-    table_lane = lax.broadcasted_iota(I32, (BOX, WIDE), 1) >> 4
-    table_row = lax.broadcasted_iota(I32, (BOX, WIDE), 0)
+    table_step = (
+        lax.broadcasted_iota(I32, (BOX, WIDE), 0)
+        - (lax.broadcasted_iota(I32, (BOX, WIDE), 1) >> 4)
+    ).astype(I16)
+    one = jnp.ones((BOX, WIDE), BF16)
     pose_row = lax.broadcasted_iota(I32, (POSES, WIDE), 0) == (
         lax.broadcasted_iota(I32, (POSES, WIDE), 1) & (POSES - 1)
     )
 
     def table_rows(g, carry):
         at = pl.ds(pl.multiple_of(g * WIDE, WIDE), WIDE)
-        chosen_row = jnp.where(table_row == table_lane + g * GROUP, 1.0, 0.0).astype(BF16)
+        first_row = jnp.full((BOX, WIDE), g * GROUP, I32).astype(I16)
+        chosen_row = jnp.where(table_step == first_row, one, jnp.zeros_like(one))
         wide = jnp.dot(tables, chosen_row, preferred_element_type=F32)
         found = [
             jnp.sum(
@@ -324,10 +326,8 @@
             weights[n, :, at] = jnp.broadcast_to(found[4 + n], (GROUP, WIDE)).astype(BF16)
         return carry
 
-    lax.fori_loop(0, 8, table_rows, 0, unroll=2)
-    pass_on(2, 6)
-    lax.fori_loop(8, BOX // GROUP, table_rows, 0, unroll=2)
-    pass_on(3, 5, 4)
+    lax.fori_loop(0, BOX // GROUP, table_rows, 0, unroll=8)
+    pass_on(1, 7)
     slot_row = lax.broadcasted_iota(I32, (GROUP, WIDE), 0).astype(I16)
 
     def spread_rows(g, carry):
@@ -345,13 +345,9 @@
                 )
         return carry
 
-    lax.fori_loop(0, 5, spread_rows, 0)
-    swap(0)
-    lax.fori_loop(5, 10, spread_rows, 0)
-    swap(1)
-    lax.fori_loop(10, BOX // GROUP, spread_rows, 0)
-
-    square = squares[...].astype(BF16)
+    lax.fori_loop(0, BOX // GROUP, spread_rows, 0)
+    pass_on(2, 6)
+
     slot_rows = lax.broadcasted_iota(I32, (GROUP, BOX), 0).astype(I16)
     for n, table, target, kind in (
         (0, first, pose_slots, I16),
@@ -374,11 +370,16 @@
             rest = jnp.where(second_slot == row, second_part, jnp.zeros_like(second_part))
             blocks.append(jnp.where(first_slot == row, first_part, rest))
         spread_square[p] = jnp.dot(
-            jnp.concatenate(blocks, axis=0), square, preferred_element_type=F32
+            jnp.concatenate(blocks, axis=0), squares[...], preferred_element_type=F32
         )
         return carry
 
-    lax.fori_loop(0, POSES, spread_squares, 0, unroll=4)
+    pass_on(3, 5, 4)
+    lax.fori_loop(0, 8, shift_rows, 0)
+    swap(0)
+    lax.fori_loop(8, BOX // GROUP, shift_rows, 0)
+    swap(1)
+    lax.fori_loop(0, POSES, spread_squares, 0, unroll=8)
     swap(2)
 
     slot_lines = held_row(lax.broadcasted_iota(I32, (1, LINES), 1), z, y, x, core)
@@ -682,7 +683,7 @@
             pltpu.VMEM((2 * BOX, ROWS), BF16),
             pltpu.VMEM((ROWS, 2 * BOX), BF16),
             pltpu.VMEM((2 * SHIFTS * SHIFTS, ROWS), BF16),
-            pltpu.VMEM((BOX, BOX), F32),
+            pltpu.VMEM((BOX, BOX), BF16),
             pltpu.VMEM((ROWS, WIDE), BF16),
             pltpu.VMEM((POSES, ROWS), BF16),
             pltpu.VMEM((ROWS, 2 * BOX), BF16),

time: 57.4 us -> 56.9 us (level)
  no operation moved by 1% of the time
where the time goes in v6:
time: 56.9 us; the launch traced here: 56.7 us
  Pallas kernels  51.1 us (90%)
  between operations  4.35 us (8%)
  local copies, waits for them, and re-layouts  0.65 us (1%)
  other arithmetic  0.58 us (1%)
    pallas_call x1, Pallas kernels, expect(): pl.pallas_call(expect_kernel, out_shape=(jax.ShapeDtypeStruct((1, 3 * BOX...  51.1 us

profile of v6, /device:TPU:8, one launch (start us, length us, event | category | flops | bytes accessed | tf_op | source)
XLA Modules:
  0.0 56.7 jit_solution(6278530145076984461)
XLA Ops:
  2.6 51.1 %shard_map.113 = (f32[1,768]{1,0:T(1,128)}, f32[1]{0:T(128)}) custom-call(s32[1]{0:T(128)S(6)} %copy.15.class_hbm, f32[1]{0:T(128)S(6)} %copy.16.precision_hbm, s32[1]{0:T(128)S(6)} %copy.17.live_hbm, f32[16]{0:T(128)} %defocus_hbm.1, s32[8]{0:T(128)} %row_shift_hbm.1, s32[8]{0:T(128)} %column_shift_hbm.1, bf16[1,2,256,256]{3,2,1,0:T(8,128)(2,1)} %image_hbm.1, ...), custom_call_target="tpu_custom_call" | custom-call | tf_op jit(solution)/shard_map/pallas_call | solution.py:664
  53.7 0.0 copy-start
  53.7 0.7 %copy-done = f32[1,768]{1,0:T(1,128)S(1)} copy-done((f32[1,768]{1,0:T(1,128)S(1)}, f32[1,768]{1,0:T(1,128)}, u32[]{:S(2)}) %copy-start) | copy-done | bytes 3096
  54.3 0.6 %broadcast_multiply_fusion = f32[1,768]{1,0:T(1,128)} fusion(f32[1,768]{1,0:T(1,128)S(1)} %copy-done), kind=kLoop, calls=%fused_computation | loop fusion | flops 768 | bytes 6144 | tf_op jit(solution)/shard_map/mul | solution.py:747
Async XLA Ops:
  53.7 0.7 %copy-start = (f32[1,768]{1,0:T(1,128)S(1)}, f32[1,768]{1,0:T(1,128)}, u32[]{:S(2)}) copy-start(f32[1,768]{1,0:T(1,128)} %get-tuple-element.4) | copy-start | bytes 9220

commit v7 on v6

--- a/solution.py
+++ b/solution.py
@@ -261,7 +261,6 @@
         shifted[at, :] = jnp.concatenate(blocks, axis=0).astype(BF16)
         return carry
 
-
     lane = lax.broadcasted_iota(I32, (SHIFTS, ROWS), 1)
     freq = (lane >> 4) - BOX // 2
     part = (lane >> 3) & 1
@@ -510,27 +509,32 @@
         both_parts = jnp.dot(parts, phases[...], preferred_element_type=F32)
         turned[...] = (both_parts[:POSES] + both_parts[POSES:]).astype(BF16)
 
-    def insert(g, carry):
-        at = pl.ds(pl.multiple_of(g * WIDE, WIDE), WIDE)
-        turns_g = turned[:, at]
-        weight = jnp.concatenate(
-            [
-                diagonal(
-                    k,
-                    jnp.where(
-                        lane_row == k % (GROUP // 2),
-                        turns_g[:, k // (GROUP // 2) * 128 : k // (GROUP // 2) * 128 + 128],
-                        nothing,
-                    ),
-                )
-                for k in range(GROUP)
-            ],
-            axis=0,
-        )
-        rows[at, :] = jnp.dot(
-            weight, shifted[at, :], preferred_element_type=F32
-        ).astype(BF16)
-        return carry
+    def insert(c):
+        columns = slice(c * BOX, (c + 1) * BOX)
+
+        def step(g, carry):
+            at = pl.ds(pl.multiple_of(g * WIDE, WIDE), WIDE)
+            turns_g = turned[:, at]
+            weight = jnp.concatenate(
+                [
+                    diagonal(
+                        k,
+                        jnp.where(
+                            lane_row == k % (GROUP // 2),
+                            turns_g[:, k // (GROUP // 2) * 128 : k // (GROUP // 2) * 128 + 128],
+                            nothing,
+                        ),
+                    )
+                    for k in range(GROUP)
+                ],
+                axis=0,
+            )
+            rows[at, columns] = jnp.dot(
+                weight, shifted[at, columns], preferred_element_type=F32
+            ).astype(BF16)
+            return carry
+
+        lax.fori_loop(0, BOX // GROUP, step, 0, unroll=True)
 
     hops = []
 
@@ -542,9 +546,11 @@
 
 
     send_pair(2, spread_mass(KEEP))
+    turn_poses()
+    insert(0)
+    send_pair(0, spread_half(KEEP, 0))
     sums[2] = spread_mass(0)
-    turn_poses()
-    lax.fori_loop(0, BOX // GROUP, insert, 0, unroll=True)
+    insert(1)
     pairs[0].wait_recv()
     c_sum = sums[2] + pair_in[2].astype(F32)
     for half in range(2):
@@ -558,10 +564,8 @@
     for k in ring8:
         cz_out[k] = c_rows(k).astype(BF16)
         c_hops.append(hop(k, cz_out.at[k], cz_in.at[k], along_z(k)))
-    send_pair(0, spread_half(KEEP, 0))
     send_pair_blocks(1, spread_half(KEEP, 1))
     spread_own(0)
-    spread_own(1)
 
     pairs[1].wait_recv()
     b_sum = (sums[0] + pair_in[0].astype(F32)).reshape(NX, NY, NZ, BOX)
@@ -570,6 +574,9 @@
         by_out[k] = b_sum[:, k].reshape(NX * NZ, BOX).astype(BF16)
         b_hops.append(hop(NZ + k, by_out.at[k], by_in.at[k], along_y(k)))
     b_sum = b_sum[:, 0].reshape(NX * NZ, BOX)
+
+    spread_own(1)
+
     def a_block(k):
         a_pairs[k].wait_recv()
         block = pl.ds(k * part, part)

time: 56.9 us -> 58.5 us (1.028)
  Pallas kernels: 51.1 us -> 52.6 us
    pallas_call x1, Pallas kernels: 51.1 us -> 52.6 us  [expect(): pl.pallas_call(expect_kernel, out_shape=(jax.ShapeDtypeStruct((1, 3 * BOX...]
where the time goes in v7:
time: 58.5 us; the launch traced here: 58.2 us
  Pallas kernels  52.6 us (90%)
  between operations  4.35 us (7%)
  local copies, waits for them, and re-layouts  0.65 us (1%)
    pallas_call x1, Pallas kernels, expect(): pl.pallas_call(expect_kernel, out_shape=(jax.ShapeDtypeStruct((1, 3 * BOX...  52.6 us

profile of v7, /device:TPU:8, one launch (start us, length us, event | category | flops | bytes accessed | tf_op | source)
XLA Modules:
  0.0 58.2 jit_solution(2413886812974089719)
XLA Ops:
  2.6 52.6 %shard_map.113 = (f32[1,768]{1,0:T(1,128)}, f32[1]{0:T(128)}) custom-call(s32[1]{0:T(128)S(6)} %copy.15.class_hbm, f32[1]{0:T(128)S(6)} %copy.16.precision_hbm, s32[1]{0:T(128)S(6)} %copy.17.live_hbm, f32[16]{0:T(128)} %defocus_hbm.1, s32[8]{0:T(128)} %row_shift_hbm.1, s32[8]{0:T(128)} %column_shift_hbm.1, bf16[1,2,256,256]{3,2,1,0:T(8,128)(2,1)} %image_hbm.1, ...), custom_call_target="tpu_custom_call" | custom-call | tf_op jit(solution)/shard_map/pallas_call | solution.py:671
  55.2 0.0 copy-start
  55.2 0.7 %copy-done = f32[1,768]{1,0:T(1,128)S(1)} copy-done((f32[1,768]{1,0:T(1,128)S(1)}, f32[1,768]{1,0:T(1,128)}, u32[]{:S(2)}) %copy-start) | copy-done | bytes 3096
  55.8 0.6 broadcast_multiply_fusion
Async XLA Ops:
  55.2 0.7 %copy-start = (f32[1,768]{1,0:T(1,128)S(1)}, f32[1,768]{1,0:T(1,128)}, u32[]{:S(2)}) copy-start(f32[1,768]{1,0:T(1,128)} %get-tuple-element.4) | copy-start | bytes 9220

commit v8 on v6

--- a/solution.py
+++ b/solution.py
@@ -13,6 +13,8 @@
 BF16 = jnp.bfloat16
 I32 = jnp.int32
 I16 = jnp.int16
+F8 = jnp.float8_e4m3fn
+LOW_SCALE = 512.0
 
 NX, NY, NZ, Y_LO = 4, 8, 8, 4
 SLABS = NZ * Y_LO
@@ -97,7 +99,9 @@
     slots,
     weights,
     lines_t,
+    lines_low,
     spread,
+    spread_low,
     slices,
     shifted,
     phases,
@@ -261,7 +265,6 @@
         shifted[at, :] = jnp.concatenate(blocks, axis=0).astype(BF16)
         return carry
 
-
     lane = lax.broadcasted_iota(I32, (SHIFTS, ROWS), 1)
     freq = (lane >> 4) - BOX // 2
     part = (lane >> 3) & 1
@@ -292,8 +295,8 @@
             (second & 15).astype(F32),
             first_high,
             second_high,
-            first_weight - first_high,
-            second_weight - second_high,
+            (first_weight - first_high) * LOW_SCALE,
+            (second_weight - second_high) * LOW_SCALE,
         ],
         axis=0,
     ).astype(BF16)
@@ -334,15 +337,25 @@
         at = pl.ds(pl.multiple_of(g * WIDE, WIDE), WIDE)
         first_slot, second_slot = slots[0, :, at], slots[1, :, at]
         parts = [weights[n, :, at] for n in range(4)]
+        lows = []
         for block in range(LINES // GROUP):
             row = slot_row + jnp.int16(block * GROUP)
             is_first = first_slot == row
             is_second = second_slot == row
-            for n, base in ((0, 0), (2, LINES)):
-                rest = jnp.where(is_second, parts[n + 1], jnp.zeros_like(parts[n]))
-                spread[base + block * GROUP : base + (block + 1) * GROUP, at] = jnp.where(
-                    is_first, parts[n], rest
+            high, low = (
+                jnp.where(
+                    is_first,
+                    parts[n],
+                    jnp.where(is_second, parts[n + 1], jnp.zeros_like(parts[n])),
                 )
+                for n in (0, 2)
+            )
+            spread[block * GROUP : (block + 1) * GROUP, at] = high
+            lows.append(low)
+            if block % 2:
+                spread_low[(block - 1) * GROUP : (block + 1) * GROUP, at] = jnp.concatenate(
+                    lows[-2:], axis=0
+                ).astype(F8)
         return carry
 
     lax.fori_loop(0, BOX // GROUP, spread_rows, 0)
@@ -388,24 +401,24 @@
     ).astype(BF16)
 
     def transpose_half(c):
+        rows_c = pl.ds(pl.multiple_of(c * BOX, BOX), BOX)
         half = lax.dot_general(
             held[c].reshape(LINES, BOX),
             order,
             (((0,), (0,)), ((), ())),
             preferred_element_type=F32,
-        ).astype(BF16)
-        lines_t[pl.ds(pl.multiple_of(c * BOX, BOX), BOX), :] = jnp.concatenate(
-            [half, half], axis=1
         )
+        lines_t[rows_c, :] = half.astype(BF16)
+        lines_low[rows_c, :] = half.astype(F8)
 
     def slice_half(c):
         half = pl.ds(pl.multiple_of(c * BOX, BOX), BOX)
 
         def step(n, carry):
             at = pl.ds(pl.multiple_of(n * 4 * WIDE, 4 * WIDE), 4 * WIDE)
-            slices[half, at] = jnp.dot(
-                lines_t[half, :], spread[:, at], preferred_element_type=F32
-            ).astype(BF16)
+            high = jnp.dot(lines_t[half, :], spread[:, at], preferred_element_type=F32)
+            low = jnp.dot(lines_low[half, :], spread_low[:, at], preferred_element_type=F32)
+            slices[half, at] = (high + low * (1.0 / LOW_SCALE)).astype(BF16)
             return carry
 
         lax.fori_loop(0, ROWS // (4 * WIDE), step, 0, unroll=True)
@@ -678,8 +691,10 @@
             pltpu.VMEM((2, Y_LO, NZ, 16, BOX), BF16),
             pltpu.VMEM((2, GROUP, ROWS), I16),
             pltpu.VMEM((4, GROUP, ROWS), BF16),
-            pltpu.VMEM((2 * BOX, 2 * LINES), BF16),
-            pltpu.VMEM((2 * LINES, ROWS), BF16),
+            pltpu.VMEM((2 * BOX, LINES), BF16),
+            pltpu.VMEM((2 * BOX, LINES), F8),
+            pltpu.VMEM((LINES, ROWS), BF16),
+            pltpu.VMEM((LINES, ROWS), F8),
             pltpu.VMEM((2 * BOX, ROWS), BF16),
             pltpu.VMEM((ROWS, 2 * BOX), BF16),
             pltpu.VMEM((2 * SHIFTS * SHIFTS, ROWS), BF16),

time: 56.9 us -> 55.9 us (0.982)
  Pallas kernels: 51.1 us -> 50.1 us
    pallas_call x1, Pallas kernels: 51.1 us -> 50.1 us  [expect(): pl.pallas_call(expect_kernel, out_shape=(jax.ShapeDtypeStruct((1, 3 * BOX...]
where the time goes in v8:
time: 55.9 us; the launch traced here: 55.6 us
  Pallas kernels  50.1 us (90%)
  between operations  4.35 us (8%)
  local copies, waits for them, and re-layouts  0.65 us (1%)
  other arithmetic  0.58 us (1%)
    pallas_call x1, Pallas kernels, expect(): pl.pallas_call(expect_kernel, out_shape=(jax.ShapeDtypeStruct((1, 3 * BOX...  50.1 us

profile of v8, /device:TPU:8, one launch (start us, length us, event | category | flops | bytes accessed | tf_op | source)
XLA Modules:
  0.0 55.6 jit_solution(16272700260834338448)
XLA Ops:
  2.6 50.1 %shard_map.113 = (f32[1,768]{1,0:T(1,128)}, f32[1]{0:T(128)}) custom-call(s32[1]{0:T(128)S(6)} %copy.15.class_hbm, f32[1]{0:T(128)S(6)} %copy.16.precision_hbm, s32[1]{0:T(128)S(6)} %copy.17.live_hbm, f32[16]{0:T(128)} %defocus_hbm.1, s32[8]{0:T(128)} %row_shift_hbm.1, s32[8]{0:T(128)} %column_shift_hbm.1, bf16[1,2,256,256]{3,2,1,0:T(8,128)(2,1)} %image_hbm.1, ...), custom_call_target="tpu_custom_call" | custom-call | tf_op jit(solution)/shard_map/pallas_call | solution.py:677
  52.6 0.0 copy-start
  52.7 0.7 %copy-done = f32[1,768]{1,0:T(1,128)S(1)} copy-done((f32[1,768]{1,0:T(1,128)S(1)}, f32[1,768]{1,0:T(1,128)}, u32[]{:S(2)}) %copy-start) | copy-done | bytes 3096
  53.3 0.6 %broadcast_multiply_fusion = f32[1,768]{1,0:T(1,128)} fusion(f32[1,768]{1,0:T(1,128)S(1)} %copy-done), kind=kLoop, calls=%fused_computation | loop fusion | flops 768 | bytes 6144 | tf_op jit(solution)/shard_map/mul | solution.py:762
Async XLA Ops:
  52.6 0.7 %copy-start = (f32[1,768]{1,0:T(1,128)S(1)}, f32[1,768]{1,0:T(1,128)}, u32[]{:S(2)}) copy-start(f32[1,768]{1,0:T(1,128)} %get-tuple-element.4) | copy-start | bytes 9220

commit v9 on v8

--- a/solution.py
+++ b/solution.py
@@ -727,7 +727,7 @@
             pltpu.SemaphoreType.REGULAR,
         ],
         compiler_params=pltpu.CompilerParams(
-            collective_id=0, has_side_effects=True, vmem_limit_bytes=60 * 1024 * 1024
+            collective_id=0, has_side_effects=True, vmem_limit_bytes=55208 * 1024
         ),
     )(*operands)
 

time: 55.9 us -> 55.8 us (level)
  no operation moved by 1% of the time
where the time goes in v9:
time: 55.8 us; the launch traced here: 55.6 us
  Pallas kernels  50 us (90%)
  between operations  4.34 us (8%)
  local copies, waits for them, and re-layouts  0.66 us (1%)
  other arithmetic  0.58 us (1%)
    pallas_call x1, Pallas kernels, expect(): pl.pallas_call(expect_kernel, out_shape=(jax.ShapeDtypeStruct((1, 3 * BOX...  50 us

profile of v9, /device:TPU:8, one launch (start us, length us, event | category | flops | bytes accessed | tf_op | source)
XLA Modules:
  0.0 55.6 jit_solution(17877195174814928915)
XLA Ops:
  2.6 0.0 copy-start
  2.6 0.0 copy-start.1
  2.6 0.0 copy-start.2
  2.6 0.6 %copy-done = f32[16]{0:T(128)S(1)} copy-done((f32[16]{0:T(128)S(1)}, f32[16]{0:T(128)}, u32[]{:S(2)}) %copy-start) | copy-done | bytes 88
  3.2 0.0 copy-done.1
  3.2 0.0 copy-done.2
  3.3 50.0 %shard_map.113 = (f32[1,768]{1,0:T(1,128)S(1)}, f32[1]{0:T(128)}) custom-call(s32[1]{0:T(128)S(6)} %copy.15.class_hbm, f32[1]{0:T(128)S(6)} %copy.16.precision_hbm, s32[1]{0:T(128)S(6)} %copy.17.live_hbm, f32[16]{0:T(128)S(1)} %copy-done, s32[8]{0:T(128)S(1)} %copy-done.1, s32[8]{0:T(128)S(1)} %copy-done.2, bf16[1,2,256,256]{3,2,1,0:T(8,128)(2,1)} %image_hbm.1, ...), custom_call_target="tpu_custom_call" | custom-call | tf_op jit(solution)/shard_map/pallas_call | solution.py:677
  53.3 0.6 %broadcast_multiply_fusion = f32[1,768]{1,0:T(1,128)} fusion(f32[1,768]{1,0:T(1,128)S(1)} %get-tuple-element.4), kind=kLoop, calls=%fused_computation | loop fusion | flops 768 | bytes 6144 | tf_op jit(solution)/shard_map/mul | solution.py:762
Async XLA Ops:
  2.6 0.7 %copy-start = (f32[16]{0:T(128)S(1)}, f32[16]{0:T(128)}, u32[]{:S(2)}) copy-start(f32[16]{0:T(128)} %defocus_hbm.1) | copy-start | bytes 196
  2.6 0.7 %copy-start.1 = (s32[8]{0:T(128)S(1)}, s32[8]{0:T(128)}, u32[]{:S(2)}) copy-start(s32[8]{0:T(128)} %row_shift_hbm.1) | copy-start | bytes 100
  2.6 0.7 %copy-start.2 = (s32[8]{0:T(128)S(1)}, s32[8]{0:T(128)}, u32[]{:S(2)}) copy-start(s32[8]{0:T(128)} %column_shift_hbm.1) | copy-start | bytes 100

commit v10 on v8

--- a/solution.py
+++ b/solution.py
@@ -554,9 +554,9 @@
         return copy
 
 
+    turn_poses()
     send_pair(2, spread_mass(KEEP))
     sums[2] = spread_mass(0)
-    turn_poses()
     lax.fori_loop(0, BOX // GROUP, insert, 0, unroll=True)
     pairs[0].wait_recv()
     c_sum = sums[2] + pair_in[2].astype(F32)

time: 55.9 us -> 56 us (level)
  no operation moved by 1% of the time
where the time goes in v10:
time: 56 us; the launch traced here: 55.7 us
  Pallas kernels  50.1 us (89%)
  between operations  4.35 us (8%)
  local copies, waits for them, and re-layouts  0.65 us (1%)
  other arithmetic  0.58 us (1%)
    pallas_call x1, Pallas kernels, expect(): pl.pallas_call(expect_kernel, out_shape=(jax.ShapeDtypeStruct((1, 3 * BOX...  50.1 us

profile of v10, /device:TPU:8, one launch (start us, length us, event | category | flops | bytes accessed | tf_op | source)
XLA Modules:
  0.0 55.7 jit_solution(9271216653905895095)
XLA Ops:
  2.6 50.1 %shard_map.113 = (f32[1,768]{1,0:T(1,128)}, f32[1]{0:T(128)}) custom-call(s32[1]{0:T(128)S(6)} %copy.15.class_hbm, f32[1]{0:T(128)S(6)} %copy.16.precision_hbm, s32[1]{0:T(128)S(6)} %copy.17.live_hbm, f32[16]{0:T(128)} %defocus_hbm.1, s32[8]{0:T(128)} %row_shift_hbm.1, s32[8]{0:T(128)} %column_shift_hbm.1, bf16[1,2,256,256]{3,2,1,0:T(8,128)(2,1)} %image_hbm.1, ...), custom_call_target="tpu_custom_call" | custom-call | tf_op jit(solution)/shard_map/pallas_call | solution.py:677
  52.7 0.0 copy-start
  52.7 0.7 %copy-done = f32[1,768]{1,0:T(1,128)S(1)} copy-done((f32[1,768]{1,0:T(1,128)S(1)}, f32[1,768]{1,0:T(1,128)}, u32[]{:S(2)}) %copy-start) | copy-done | bytes 3096
  53.4 0.6 %broadcast_multiply_fusion = f32[1,768]{1,0:T(1,128)} fusion(f32[1,768]{1,0:T(1,128)S(1)} %copy-done), kind=kLoop, calls=%fused_computation | loop fusion | flops 768 | bytes 6144 | tf_op jit(solution)/shard_map/mul | solution.py:762
Async XLA Ops:
  52.7 0.7 %copy-start = (f32[1,768]{1,0:T(1,128)S(1)}, f32[1,768]{1,0:T(1,128)}, u32[]{:S(2)}) copy-start(f32[1,768]{1,0:T(1,128)} %get-tuple-element.4) | copy-start | bytes 9220
